TPU v7x, 128 devices: a whole 4x4x4 slice. The times are simulated.
128 devices in a mesh: gx: 4 (over x), gy: 32 (over z, y, core).
Axes of the slice: x: 4, y: 4, z: 4, core: 2. Of those that a mesh axis runs over, the one named last changes fastest.
Arguments:
- right_side: float32 [8, 3, 64, 4096], P(None, None, 'gx', 'gy'), may hold values from -50 to 50
- first_guess: float32 [8, 3, 64, 4096], P(None, None, 'gx', 'gy'), may hold values from -3 to 3
- diag_block: bfloat16 [8, 3, 3, 64, 4096], P(None, None, None, 'gx', 'gy'), may hold values from -2.41 to 12
- mobility: bfloat16 [8, 3, 3, 64, 4096], P(None, None, None, 'gx', 'gy'), may hold values from -1 to 1.21
- face_trans: bfloat16 [6, 8, 64, 4096], P(None, None, 'gx', 'gy'), may hold values from 0.19921875 to 1
- column_inverse: bfloat16 [4, 6, 6, 64, 4096], P(None, None, None, 'gx', 'gy'), may hold values from -0.061 to 0.201
- perf_cell: int32 [128, 128, 10], P(('gx', 'gy')), may hold values from 0 to 16383, as said below
- perf_slot: int32 [128, 128, 10], P(('gx', 'gy')), may hold values from 0 to 1024, as said below
- well_in: float32 [3, 131072], P(None, ('gx', 'gy')), may hold values from -4 to 4
- well_out: float32 [3, 131072], P(None, ('gx', 'gy')), may hold values from -4 to 4
- well_inverse: float32 [1024, 128, 128], P(('gx', 'gy')), may hold values from -1 to 1
Outputs:
- solution: float32 [8, 3, 64, 4096], P(None, None, 'gx', 'gy')
- residual: float32 [8, 3, 64, 4096], P(None, None, 'gx', 'gy')
Inputs may be any that keep to these rules, and one draw needn't show every extreme that they name: `perf_cell`: entry [s, d, q] is a local cell number of device s's tile, the cell of slot q from device s to owner d; the slot's segment is perf_slot[d, s, q]; slots that perf_slot marks empty carry an arbitrary cell. `perf_slot`: entry [d, s, q] is w * 128 + g when slot q from device s carries segment g of owner d's local well w, and 1024 when the slot is empty. Each segment of an owner appears at most once; the segments of a well that appear are 0 to n - 1 for its padded count n of 1 to 128. Every pair (d, s) has at most 10 live slots and some pair has exactly 10; in every draw some owner has all 1024 segments live.
All inputs are finite; a program needn't handle non-finite values.
Results may differ from a plain program's by a relative error of at most 0.0003.
Values sent between devices are 32-bit elements; how exact they have to be, the bound alone decides.
A program may use at most 128 MiB of HBM per device.

v0:
```python
import jax
import jax.numpy as jnp
from jax import lax
from jax.sharding import PartitionSpec as P

ITERS = 2


def padded_2(block, sides, width):
    for axis, dim in sides:
        count = lax.axis_size(axis)
        forward = [(i, i + 1) for i in range(count - 1)]
        backward = [(target, source) for source, target in forward]
        low = lax.ppermute(
            lax.slice_in_dim(block, block.shape[dim] - width, None, axis=dim), axis, forward
        )
        high = lax.ppermute(lax.slice_in_dim(block, 0, width, axis=dim), axis, backward)
        block = jnp.concatenate([low, block, high], axis=dim)
    return block


def couple(mixing, vector):
    summed = mixing[:, :, 0].astype(jnp.float32) * vector[:, 0:1]
    summed = summed + mixing[:, :, 1].astype(jnp.float32) * vector[:, 1:2]
    summed = summed + mixing[:, :, 2].astype(jnp.float32) * vector[:, 2:3]
    return summed


def stencil(vector, extended, diag_block, face_trans):
    factor = face_trans.astype(jnp.float32)[:, :, None]
    interior = extended[:, :, 1:-1, 1:-1]
    zero_layer = jnp.zeros_like(interior[:1])
    under_layer = jnp.concatenate([zero_layer, interior[:-1]], axis=0)
    over_layer = jnp.concatenate([interior[1:], zero_layer], axis=0)
    beside = factor[0] * extended[:, :, :-2, 1:-1]
    beside = beside + factor[1] * extended[:, :, 2:, 1:-1]
    beside = beside + factor[2] * extended[:, :, 1:-1, :-2]
    beside = beside + factor[3] * extended[:, :, 1:-1, 2:]
    beside = beside + factor[4] * under_layer
    beside = beside + factor[5] * over_layer
    return couple(diag_block, vector) - beside


def precondition(vector, column_inverse):
    layers, comps, tile_rows, tile_cols = vector.shape
    paired = vector.reshape(layers // 2, 6, tile_rows, tile_cols)
    result = column_inverse[:, :, 0].astype(jnp.float32) * paired[:, 0:1]
    for member in range(1, 6):
        result = (
            result
            + column_inverse[:, :, member].astype(jnp.float32) * paired[:, member : member + 1]
        )
    return result.reshape(vector.shape)


def per_device(
    right_side,
    first_guess,
    diag_block,
    mobility,
    face_trans,
    column_inverse,
    perf_cell,
    perf_slot,
    well_in,
    well_out,
    well_inverse,
):
    layers, comps, tile_rows, tile_cols = right_side.shape
    tile_area = tile_rows * tile_cols
    cell_ids = perf_cell[0]
    targets = perf_slot[0]
    layer_idx = cell_ids // tile_area
    column_idx = cell_ids % tile_area
    well_count = well_inverse.shape[0]
    seg_count = well_inverse.shape[1]
    per_owner = well_count * seg_count
    pad_in = jnp.concatenate([well_in, jnp.zeros((3, 1), jnp.float32)], axis=1)
    pad_out = jnp.concatenate([well_out, jnp.zeros((3, 1), jnp.float32)], axis=1)

    def solve_wells(rate):
        totals = jnp.zeros((per_owner + 1,), jnp.float32).at[targets].add(rate)
        seg_rate = jnp.einsum(
            "wgh,wh->wg",
            well_inverse,
            totals[:per_owner].reshape(well_count, seg_count),
            precision=lax.Precision.HIGHEST,
        )
        padded = jnp.concatenate([seg_rate.reshape(-1), jnp.zeros((1,), jnp.float32)])
        return padded[targets]

    def well_term(vector):
        flattened = vector.reshape(layers, comps, tile_area)
        values = flattened[layer_idx, :, column_idx]
        outgoing = jnp.moveaxis(values, 2, 0)
        arrived = lax.all_to_all(outgoing, ("gx", "gy"), split_axis=1, concat_axis=1, tiled=True)
        coeff_in = pad_in[:, targets]
        rate = coeff_in[0] * arrived[0] + coeff_in[1] * arrived[1] + coeff_in[2] * arrived[2]
        back = solve_wells(rate)
        terms = lax.all_to_all(
            pad_out[:, targets] * back[None], ("gx", "gy"), split_axis=1, concat_axis=1, tiled=True
        )
        scattered = (
            jnp.zeros((layers, comps, tile_area), jnp.float32)
            .at[layer_idx, :, column_idx]
            .add(jnp.moveaxis(terms, 0, 2))
        )
        return scattered.reshape(vector.shape)

    def apply_operator(vector):
        flux = couple(mobility, vector)
        extended = padded_2(flux, (("gx", 2), ("gy", 3)), 1)
        return stencil(vector, extended, diag_block, face_trans) - well_term(vector)

    iterate = first_guess
    residual = right_side - apply_operator(iterate)
    shadow = residual
    inner_now = lax.psum(jnp.sum(shadow * residual), ("gx", "gy"))
    search = residual
    for iteration in range(ITERS):
        search_hat = precondition(search, column_inverse)
        applied = apply_operator(search_hat)
        projected = lax.psum(jnp.sum(shadow * applied), ("gx", "gy"))
        step_size = inner_now / projected
        halfway = residual - step_size * applied
        halfway_hat = precondition(halfway, column_inverse)
        response = apply_operator(halfway_hat)
        cross_term, self_term = lax.psum(
            (jnp.sum(response * halfway), jnp.sum(response * response)), ("gx", "gy")
        )
        smoothing = cross_term / self_term
        iterate = iterate + step_size * search_hat + smoothing * halfway_hat
        residual = halfway - smoothing * response
        if iteration + 1 < ITERS:
            inner_next = lax.psum(jnp.sum(shadow * residual), ("gx", "gy"))
            momentum = inner_next / inner_now * (step_size / smoothing)
            search = residual + momentum * (search - smoothing * applied)
            inner_now = inner_next
    return (iterate, right_side - apply_operator(iterate))


def solution(mesh):
    in_specs = (
        P(None, None, "gx", "gy"),
        P(None, None, "gx", "gy"),
        P(None, None, None, "gx", "gy"),
        P(None, None, None, "gx", "gy"),
        P(None, None, "gx", "gy"),
        P(None, None, None, "gx", "gy"),
        P(("gx", "gy"), None, None),
        P(("gx", "gy"), None, None),
        P(None, ("gx", "gy")),
        P(None, ("gx", "gy")),
        P(("gx", "gy"), None, None),
    )
    out_specs = (P(None, None, "gx", "gy"), P(None, None, "gx", "gy"))
    return jax.shard_map(
        per_device, mesh=mesh, in_specs=in_specs, out_specs=out_specs, check_vma=False
    )
```

profile of v0, /device:TPU:1, one launch (start us, length us, event | category | flops | bytes accessed | tf_op | source)
XLA Modules:
  0.0 991.2 jit_solution(2833501067635090127)
XLA Ops:
  7.4 9.6 gather_fusion.2
  18.2 12.0 %all-to-all-start = ((f32[3,128,10]{2,0,1:T(4,128)}), f32[3,128,10]{2,0,1:T(4,128)}, u32[]{:S(2)}, u32[]{:S(2)}) async-start(f32[3,128,10]{2,0,1:T(4,128)} %copy.332), calls=%async_computation | async-start | bytes 524288 | tf_op jit(solution)/shard_map/all_to_all | solution.py:96
  77.6 11.0 %all-to-all-start.1 = ((f32[3,128,10]{2,0,1:T(4,128)}), f32[3,128,10]{2,0,1:T(4,128)S(1)}, u32[]{:S(2)}, u32[]{:S(2)}) async-start(f32[3,128,10]{2,0,1:T(4,128)} %copy.336), calls=%async_computation.1 | async-start | bytes 524288 | tf_op jit(solution)/shard_map/all_to_all | solution.py:100
  102.2 13.0 %scatter_custom_fusion.6 = f32[3,16384]{0,1:T(8,128)} fusion(s32[1280]{0:T(1024)S(1)} %reshape.628, f32[1280,3]{1,0:T(8,128)} %copy.338, f32[]{:T(128)} %constant.32.clone.1), kind=kCustom, calls=%fused_computation.36 | custom fusion | flops 3840 | bytes 197120
  139.4 12.7 %gather_fusion.4 = f32[1280,3]{1,0:T(8,128)} fusion(f32[8,3,2048]{1,2,0:T(8,128)} %copy.360, s32[1280]{0:T(1024)S(1)} %reshape.496), kind=kCustom, calls=%fused_computation.4 | custom fusion | bytes 40960 | tf_op jit(solution)/shard_map/gather | solution.py:94
  193.7 9.1 all-to-all-start.3
  217.3 13.0 %scatter_custom_fusion.7 = f32[3,16384]{0,1:T(8,128)} fusion(s32[1280]{0:T(1024)} %copy-done.66, f32[1280,3]{1,0:T(8,128)} %copy.368, f32[]{:T(128)} %constant.32.clone.1), kind=kCustom, calls=%fused_computation.34 | custom fusion | flops 3840 | bytes 197120
  239.6 63.0 %all-reduce.16 = (f32[]{:T(128)}, f32[]{:T(128)}) all-reduce(f32[]{:T(128)} %get-tuple-element.15, f32[]{:T(128)} %get-tuple-element.14), channel_id=1, replica_groups=mesh['gx'=4,'gy'=32] {'gx','gy'}, use_global_device_ids=true, to_apply=%region_3.4 | all-reduce | flops 2 | bytes 16 | tf_op jit(solution)/shard_map/psum | solution.py:118
  320.6 12.7 %gather_fusion.6 = f32[1280,3]{1,0:T(8,128)} fusion(f32[8,3,2048]{1,2,0:T(8,128)} %copy.384, s32[1280]{0:T(1024)S(1)} %reshape.496), kind=kCustom, calls=%fused_computation.6 | custom fusion | bytes 40960 | tf_op jit(solution)/shard_map/gather | solution.py:94
  371.8 9.5 all-to-all-start.5
  395.7 13.0 %scatter_custom_fusion.8 = f32[3,16384]{0,1:T(8,128)} fusion(s32[1280]{0:T(1024)} %copy-done.66, f32[1280,3]{1,0:T(8,128)} %copy.392, f32[]{:T(128)} %constant.32.clone.1), kind=kCustom, calls=%fused_computation.32 | custom fusion | flops 3840 | bytes 197120
  418.1 63.0 %all-reduce.15 = (f32[]{:T(128)}, f32[]{:T(128)}) all-reduce(f32[]{:T(128)} %get-tuple-element.13, f32[]{:T(128)} %get-tuple-element.12), channel_id=1, replica_groups=mesh['gx'=4,'gy'=32] {'gx','gy'}, use_global_device_ids=true, to_apply=%region_11.12 | all-reduce | flops 2 | bytes 16 | tf_op jit(solution)/shard_map/psum | solution.py:128
  486.7 63.0 %psum.60 = f32[]{:T(128)} all-reduce(f32[]{:T(128)} %multiply_reduce_fusion.3), channel_id=1, replica_groups=mesh['gx'=4,'gy'=32] {'gx','gy'}, use_global_device_ids=true, to_apply=%region_15.16 | all-reduce | flops 1 | bytes 8 | tf_op jit(solution)/shard_map/psum | solution.py:135
  568.6 12.7 %gather_fusion.8 = f32[1280,3]{1,0:T(8,128)} fusion(f32[8,3,2048]{1,2,0:T(8,128)} %copy.407, s32[1280]{0:T(1024)S(1)} %reshape.496), kind=kCustom, calls=%fused_computation.8 | custom fusion | bytes 40960 | tf_op jit(solution)/shard_map/gather | solution.py:94
  622.7 9.1 all-to-all-start.7
  646.2 13.0 %scatter_custom_fusion.9 = f32[3,16384]{0,1:T(8,128)} fusion(s32[1280]{0:T(1024)} %copy-done.66, f32[1280,3]{1,0:T(8,128)} %copy.415, f32[]{:T(128)} %constant.32.clone.1), kind=kCustom, calls=%fused_computation.30 | custom fusion | flops 3840 | bytes 197120
  668.6 63.2 %psum.61 = f32[]{:T(128)} all-reduce(f32[]{:T(128)} %get-tuple-element.22), channel_id=1, replica_groups=mesh['gx'=4,'gy'=32] {'gx','gy'}, use_global_device_ids=true, to_apply=%region_19.20 | all-reduce | flops 1 | bytes 8 | tf_op jit(solution)/shard_map/psum | solution.py:123
  748.0 9.6 gather_fusion.10
  799.8 10.0 %all-to-all-done.9 = f32[3,128,10]{2,0,1:T(4,128)S(1)} async-done(((f32[3,128,10]{2,0,1:T(4,128)}), f32[3,128,10]{2,0,1:T(4,128)S(1)}, u32[]{:S(2)}, u32[]{:S(2)}) %all-to-all-start.9) | async-done | bytes 15392 | tf_op jit(solution)/shard_map/all_to_all | solution.py:100
  811.2 13.4 %scatter_custom_fusion.10 = f32[3,16384]{0,1:T(8,128)} fusion(s32[1280]{0:T(1024)} %copy-done.66, f32[1280,3]{1,0:T(8,128)} %copy.438, f32[]{:T(128)} %constant.32.clone.1), kind=kCustom, calls=%fused_computation.28 | custom fusion | flops 3840 | bytes 197120
  833.1 63.2 %all-reduce.14 = (f32[]{:T(128)}, f32[]{:T(128)}) all-reduce(f32[]{:T(128)} %get-tuple-element.11, f32[]{:T(128)} %get-tuple-element.10), channel_id=1, replica_groups=mesh['gx'=4,'gy'=32] {'gx','gy'}, use_global_device_ids=true, to_apply=%region_23.24 | all-reduce | flops 2 | bytes 16 | tf_op jit(solution)/shard_map/psum | solution.py:128
  908.0 9.6 gather_fusion.12
  960.1 10.0 %all-to-all-done.11 = f32[3,128,10]{2,0,1:T(4,128)S(1)} async-done(((f32[3,128,10]{2,0,1:T(4,128)}), f32[3,128,10]{2,0,1:T(4,128)S(1)}, u32[]{:S(2)}, u32[]{:S(2)}) %all-to-all-start.11) | async-done | bytes 15392 | tf_op jit(solution)/shard_map/all_to_all | solution.py:100
  970.6 12.9 %scatter_custom_fusion.11 = f32[3,16384]{0,1:T(8,128)} fusion(s32[1280]{0:T(1024)} %copy-done.66, f32[1280,3]{1,0:T(8,128)S(1)} %copy.448, f32[]{:T(128)} %constant.32.clone.1), kind=kCustom, calls=%fused_computation.26 | custom fusion | flops 3840 | bytes 197120
  (462 shorter events, 447.4 us)
Async XLA Ops:
  18.2 41.4 %all-to-all-start = ((f32[3,128,10]{2,0,1:T(4,128)}), f32[3,128,10]{2,0,1:T(4,128)}, u32[]{:S(2)}, u32[]{:S(2)}) async-start(f32[3,128,10]{2,0,1:T(4,128)} %copy.332), calls=%async_computation | async-start | bytes 524288 | tf_op jit(solution)/shard_map/all_to_all | solution.py:96
  53.6 67.5 %collective-permute-start.3 = (f32[8,3,18,1]{3,2,0,1:T(8,128)}, f32[8,3,18,1]{3,2,0,1:T(8,128)}, u32[]{:S(2)}, u32[]{:S(2)}) collective-permute-start(f32[8,3,18,1]{3,2,0,1:T(8,128)} %get-tuple-element.55), channel_id=1, source_target_pairs={{1,0},{2,1},{3,2},{4,3},{5,4},{6,5},{7,6},{8,7},{9,8},{10,9},{11,1... | collective-permute-start | bytes 5192 | tf_op jit(solution)/shard_map/ppermute | solution.py:17
  57.2 63.9 %collective-permute-start.2 = (f32[8,3,18,1]{3,2,0,1:T(8,128)}, f32[8,3,18,1]{3,2,0,1:T(8,128)}, u32[]{:S(2)}, u32[]{:S(2)}) collective-permute-start(f32[8,3,18,1]{3,2,0,1:T(8,128)} %get-tuple-element.54), channel_id=1, source_target_pairs={{0,1},{1,2},{2,3},{3,4},{4,5},{5,6},{6,7},{7,8},{8,9},{9,10},{10,1... | collective-permute-start | bytes 5192 | tf_op jit(solution)/shard_map/ppermute | solution.py:14
  77.6 21.7 %all-to-all-start.1 = ((f32[3,128,10]{2,0,1:T(4,128)}), f32[3,128,10]{2,0,1:T(4,128)S(1)}, u32[]{:S(2)}, u32[]{:S(2)}) async-start(f32[3,128,10]{2,0,1:T(4,128)} %copy.336), calls=%async_computation.1 | async-start | bytes 524288 | tf_op jit(solution)/shard_map/all_to_all | solution.py:100
  125.9 36.1 %collective-permute-start.5 = (f32[8,3,1,128]{3,2,0,1:T(1,128)}, f32[8,3,1,128]{3,2,0,1:T(1,128)S(1)}, u32[]{:S(2)}, u32[]{:S(2)}) collective-permute-start(f32[8,3,1,128]{3,2,0,1:T(1,128)} %get-tuple-element.124), channel_id=1, source_target_pairs={{32,0},{64,32},{96,64},{33,1},{65,33},{97,65},{34,2},{66,34},{98,6... | collective-permute-start | bytes 36872 | tf_op jit(solution)/shard_map/ppermute | solution.py:17
  127.2 34.8 %collective-permute-start.4 = (f32[8,3,1,128]{3,2,0,1:T(1,128)}, f32[8,3,1,128]{3,2,0,1:T(1,128)S(1)}, u32[]{:S(2)}, u32[]{:S(2)}) collective-permute-start(f32[8,3,1,128]{3,2,0,1:T(1,128)} %get-tuple-element.123), channel_id=1, source_target_pairs={{0,32},{32,64},{64,96},{1,33},{33,65},{65,97},{2,34},{34,66},{66,9... | collective-permute-start | bytes 36872 | tf_op jit(solution)/shard_map/ppermute | solution.py:14
  163.9 72.2 %collective-permute-start.7 = (f32[8,3,18,1]{3,2,0,1:T(8,128)}, f32[8,3,18,1]{3,2,0,1:T(8,128)}, u32[]{:S(2)}, u32[]{:S(2)}) collective-permute-start(f32[8,3,18,1]{3,2,0,1:T(8,128)} %get-tuple-element.50), channel_id=1, source_target_pairs={{1,0},{2,1},{3,2},{4,3},{5,4},{6,5},{7,6},{8,7},{9,8},{10,9},{11,1... | collective-permute-start | bytes 5192 | tf_op jit(solution)/shard_map/ppermute | solution.py:17
  167.1 69.0 %collective-permute-start.6 = (f32[8,3,18,1]{3,2,0,1:T(8,128)}, f32[8,3,18,1]{3,2,0,1:T(8,128)}, u32[]{:S(2)}, u32[]{:S(2)}) collective-permute-start(f32[8,3,18,1]{3,2,0,1:T(8,128)} %get-tuple-element.49), channel_id=1, source_target_pairs={{0,1},{1,2},{2,3},{3,4},{4,5},{5,6},{6,7},{7,8},{8,9},{9,10},{10,1... | collective-permute-start | bytes 5192 | tf_op jit(solution)/shard_map/ppermute | solution.py:14
  307.2 35.9 %collective-permute-start.9 = (f32[8,3,1,128]{3,2,0,1:T(1,128)S(1)}, f32[8,3,1,128]{3,2,0,1:T(1,128)S(1)}, u32[]{:S(2)}, u32[]{:S(2)}) collective-permute-start(f32[8,3,1,128]{3,2,0,1:T(1,128)S(1)} %get-tuple-element.111), channel_id=1, source_target_pairs={{32,0},{64,32},{96,64},{33,1},{65,33},{97,65},{34,2},{66,34},{98,6... | collective-permute-start | bytes 36872 | tf_op jit(solution)/shard_map/ppermute | solution.py:17
  308.6 34.6 %collective-permute-start.8 = (f32[8,3,1,128]{3,2,0,1:T(1,128)S(1)}, f32[8,3,1,128]{3,2,0,1:T(1,128)S(1)}, u32[]{:S(2)}, u32[]{:S(2)}) collective-permute-start(f32[8,3,1,128]{3,2,0,1:T(1,128)S(1)} %get-tuple-element.110), channel_id=1, source_target_pairs={{0,32},{32,64},{64,96},{1,33},{33,65},{65,97},{2,34},{34,66},{66,9... | collective-permute-start | bytes 36872 | tf_op jit(solution)/shard_map/ppermute | solution.py:14
  345.1 69.5 %collective-permute-start.11 = (f32[8,3,18,1]{3,2,0,1:T(8,128)}, f32[8,3,18,1]{3,2,0,1:T(8,128)}, u32[]{:S(2)}, u32[]{:S(2)}) collective-permute-start(f32[8,3,18,1]{3,2,0,1:T(8,128)} %get-tuple-element.48), channel_id=1, source_target_pairs={{1,0},{2,1},{3,2},{4,3},{5,4},{6,5},{7,6},{8,7},{9,8},{10,9},{11,1... | collective-permute-start | bytes 5192 | tf_op jit(solution)/shard_map/ppermute | solution.py:17
  348.3 66.3 %collective-permute-start.10 = (f32[8,3,18,1]{3,2,0,1:T(8,128)}, f32[8,3,18,1]{3,2,0,1:T(8,128)}, u32[]{:S(2)}, u32[]{:S(2)}) collective-permute-start(f32[8,3,18,1]{3,2,0,1:T(8,128)} %get-tuple-element.47), channel_id=1, source_target_pairs={{0,1},{1,2},{2,3},{3,4},{4,5},{5,6},{6,7},{7,8},{8,9},{9,10},{10,1... | collective-permute-start | bytes 5192 | tf_op jit(solution)/shard_map/ppermute | solution.py:14
  555.1 36.1 %collective-permute-start.13 = (f32[8,3,1,128]{3,2,0,1:T(1,128)}, f32[8,3,1,128]{3,2,0,1:T(1,128)S(1)}, u32[]{:S(2)}, u32[]{:S(2)}) collective-permute-start(f32[8,3,1,128]{3,2,0,1:T(1,128)} %get-tuple-element.98), channel_id=1, source_target_pairs={{32,0},{64,32},{96,64},{33,1},{65,33},{97,65},{34,2},{66,34},{98,6... | collective-permute-start | bytes 36872 | tf_op jit(solution)/shard_map/ppermute | solution.py:17
  556.4 34.8 %collective-permute-start.12 = (f32[8,3,1,128]{3,2,0,1:T(1,128)}, f32[8,3,1,128]{3,2,0,1:T(1,128)S(1)}, u32[]{:S(2)}, u32[]{:S(2)}) collective-permute-start(f32[8,3,1,128]{3,2,0,1:T(1,128)} %get-tuple-element.97), channel_id=1, source_target_pairs={{0,32},{32,64},{64,96},{1,33},{33,65},{65,97},{2,34},{34,66},{66,9... | collective-permute-start | bytes 36872 | tf_op jit(solution)/shard_map/ppermute | solution.py:14
  593.2 71.8 %collective-permute-start.15 = (f32[8,3,18,1]{3,2,0,1:T(8,128)}, f32[8,3,18,1]{3,2,0,1:T(8,128)}, u32[]{:S(2)}, u32[]{:S(2)}) collective-permute-start(f32[8,3,18,1]{3,2,0,1:T(8,128)} %get-tuple-element.46), channel_id=1, source_target_pairs={{1,0},{2,1},{3,2},{4,3},{5,4},{6,5},{7,6},{8,7},{9,8},{10,9},{11,1... | collective-permute-start | bytes 5192 | tf_op jit(solution)/shard_map/ppermute | solution.py:17
  596.2 68.8 %collective-permute-start.14 = (f32[8,3,18,1]{3,2,0,1:T(8,128)}, f32[8,3,18,1]{3,2,0,1:T(8,128)}, u32[]{:S(2)}, u32[]{:S(2)}) collective-permute-start(f32[8,3,18,1]{3,2,0,1:T(8,128)} %get-tuple-element.45), channel_id=1, source_target_pairs={{0,1},{1,2},{2,3},{3,4},{4,5},{5,6},{6,7},{7,8},{8,9},{9,10},{10,1... | collective-permute-start | bytes 5192 | tf_op jit(solution)/shard_map/ppermute | solution.py:14
  736.2 27.8 %collective-permute-start.17 = (f32[8,3,1,128]{3,2,0,1:T(1,128)S(1)}, f32[8,3,1,128]{3,2,0,1:T(1,128)S(1)}, u32[]{:S(2)}, u32[]{:S(2)}) collective-permute-start(f32[8,3,1,128]{3,2,0,1:T(1,128)S(1)} %get-tuple-element.87), channel_id=1, source_target_pairs={{32,0},{64,32},{96,64},{33,1},{65,33},{97,65},{34,2},{66,34},{98,6... | collective-permute-start | bytes 36872 | tf_op jit(solution)/shard_map/ppermute | solution.py:17
  737.5 26.5 %collective-permute-start.16 = (f32[8,3,1,128]{3,2,0,1:T(1,128)S(1)}, f32[8,3,1,128]{3,2,0,1:T(1,128)S(1)}, u32[]{:S(2)}, u32[]{:S(2)}) collective-permute-start(f32[8,3,1,128]{3,2,0,1:T(1,128)S(1)} %get-tuple-element.86), channel_id=1, source_target_pairs={{0,32},{32,64},{64,96},{1,33},{33,65},{65,97},{2,34},{34,66},{66,9... | collective-permute-start | bytes 36872 | tf_op jit(solution)/shard_map/ppermute | solution.py:14
  765.0 65.6 %collective-permute-start.19 = (f32[8,3,18,1]{3,2,0,1:T(8,128)}, f32[8,3,18,1]{3,2,0,1:T(8,128)}, u32[]{:S(2)}, u32[]{:S(2)}) collective-permute-start(f32[8,3,18,1]{3,2,0,1:T(8,128)} %get-tuple-element.44), channel_id=1, source_target_pairs={{1,0},{2,1},{3,2},{4,3},{5,4},{6,5},{7,6},{8,7},{9,8},{10,9},{11,1... | collective-permute-start | bytes 5192 | tf_op jit(solution)/shard_map/ppermute | solution.py:17
  768.0 62.6 %collective-permute-start.18 = (f32[8,3,18,1]{3,2,0,1:T(8,128)}, f32[8,3,18,1]{3,2,0,1:T(8,128)}, u32[]{:S(2)}, u32[]{:S(2)}) collective-permute-start(f32[8,3,18,1]{3,2,0,1:T(8,128)} %get-tuple-element.43), channel_id=1, source_target_pairs={{0,1},{1,2},{2,3},{3,4},{4,5},{5,6},{6,7},{7,8},{8,9},{9,10},{10,1... | collective-permute-start | bytes 5192 | tf_op jit(solution)/shard_map/ppermute | solution.py:14
  898.0 26.1 %collective-permute-start.21 = (f32[8,3,1,128]{3,2,0,1:T(1,128)S(1)}, f32[8,3,1,128]{3,2,0,1:T(1,128)S(1)}, u32[]{:S(2)}, u32[]{:S(2)}) collective-permute-start(f32[8,3,1,128]{3,2,0,1:T(1,128)S(1)} %get-tuple-element.80), channel_id=1, source_target_pairs={{32,0},{64,32},{96,64},{33,1},{65,33},{97,65},{34,2},{66,34},{98,6... | collective-permute-start | bytes 36872 | tf_op jit(solution)/shard_map/ppermute | solution.py:17
  899.3 24.8 %collective-permute-start.20 = (f32[8,3,1,128]{3,2,0,1:T(1,128)S(1)}, f32[8,3,1,128]{3,2,0,1:T(1,128)S(1)}, u32[]{:S(2)}, u32[]{:S(2)}) collective-permute-start(f32[8,3,1,128]{3,2,0,1:T(1,128)S(1)} %get-tuple-element.79), channel_id=1, source_target_pairs={{0,32},{32,64},{64,96},{1,33},{33,65},{65,97},{2,34},{34,66},{66,9... | collective-permute-start | bytes 36872 | tf_op jit(solution)/shard_map/ppermute | solution.py:14
  925.1 63.7 %collective-permute-start.23 = (f32[8,3,18,1]{3,2,0,1:T(8,128)}, f32[8,3,18,1]{3,2,0,1:T(8,128)}, u32[]{:S(2)}, u32[]{:S(2)}) collective-permute-start(f32[8,3,18,1]{3,2,0,1:T(8,128)} %get-tuple-element.42), channel_id=1, source_target_pairs={{1,0},{2,1},{3,2},{4,3},{5,4},{6,5},{7,6},{8,7},{9,8},{10,9},{11,1... | collective-permute-start | bytes 5192 | tf_op jit(solution)/shard_map/ppermute | solution.py:17
  928.0 60.7 %collective-permute-start.22 = (f32[8,3,18,1]{3,2,0,1:T(8,128)}, f32[8,3,18,1]{3,2,0,1:T(8,128)}, u32[]{:S(2)}, u32[]{:S(2)}) collective-permute-start(f32[8,3,18,1]{3,2,0,1:T(8,128)} %get-tuple-element.41), channel_id=1, source_target_pairs={{0,1},{1,2},{2,3},{3,4},{4,5},{5,6},{6,7},{7,8},{8,9},{9,10},{10,1... | collective-permute-start | bytes 5192 | tf_op jit(solution)/shard_map/ppermute | solution.py:14
  (82 other events, 2190.4 us)
where the time goes:
time: 1000 us; the launch traced here: 991 us
  blocking collectives  315 us (32%)
  local copies, waits for them, and re-layouts  258 us (26%)
  other arithmetic  167 us (17%)
  starting transfers between devices  161 us (16%)
  waiting for transfers between devices  71.8 us (7%)
  between operations  12.6 us (1%)
    psum x2, blocking collectives, per_device(): lax.psum((jnp.sum(response * halfway), jnp.sum(response * response)), ('g...  126 us
    unnamed x9, other arithmetic  78.4 us
    gather x18, local copies, waits for them, and re-layouts, well_term(): values = flattened[layer_idx, :, column_idx]  74.6 us
    psum x1, blocking collectives, per_device(): projected = lax.psum(jnp.sum(shadow * applied), ('gx', 'gy'))  63.2 us
    psum x1, blocking collectives, per_device(): inner_next = lax.psum(jnp.sum(shadow * residual), ('gx', 'gy'))  63 us
    psum x1, blocking collectives, per_device(): inner_now = lax.psum(jnp.sum(shadow * residual), ('gx', 'gy'))  63 us
    all_to_all x6, waiting for transfers between devices, well_term(): lax.all_to_all(pad_out[:, targets] * back[None], ('gx', 'gy'), split_axis...  54.3 us
    all_to_all x6, starting transfers between devices, well_term(): lax.all_to_all(pad_out[:, targets] * back[None], ('gx', 'gy'), split_axis...  54 us
  transfers between devices with their start and end apart: 36, of which 11 were waited for; matrix products, arithmetic and copies ran while one was open for 38% of the time, Pallas kernels for 0%

commit v1 on v0

v1 whole, which is shorter than its diff:
```python
import jax
import jax.numpy as jnp
from jax import lax
from jax.experimental import pallas as pl
from jax.experimental.pallas import tpu as pltpu
from jax.sharding import PartitionSpec as P

MESH = pl.DeviceIdType.MESH
F32 = jnp.float32
BF16 = jnp.bfloat16
DEV = 128
CAP = 10
SLOTS = DEV * CAP
OPS = 5
EXCHANGES = 2 * OPS + 1


def dot(a, b):
    return lax.dot_general(a, b, (((1,), (0,)), ((), ())), preferred_element_type=F32)


def dot_nt(a, b):
    return lax.dot_general(a, b, (((1,), (1,)), ((), ())), preferred_element_type=F32)


def split(value):
    high = value.astype(BF16).astype(F32)
    return high, value - high


def flat(value):
    return value.reshape(128, 128)


def local_sum(lefts, rights):
    total = lefts[0] * rights[0] + lefts[1] * rights[1] + lefts[2] * rights[2]
    return jnp.sum(jnp.sum(total, axis=0, keepdims=True), axis=1, keepdims=True)


def kernel(
    right_ref, guess_ref, diag_ref, mob_ref, face_ref, colinv_ref, cell_ref, slot_ref, win_ref,
    wout_ref, winv_ref, sol_ref, res_ref,
    snd, rcv, flux_pad, col_snd, col_rcv, mt, pads, faces, oht, cmt, gts, gt, wmask, w2, vals, coef,
    snd_sem, rcv_sem, hs_sem, hr_sem,
):
    gx = lax.axis_index("gx")
    gy = lax.axis_index("gy")
    me = gx * 32 + gy
    pz, py, pc = gy // 8, (gy // 2) % 4, gy % 2

    def peer(i):
        tx, tz, ty = 3 - i // 32, 3 - (i // 8) % 4, 3 - (i // 2) % 4
        ox, oz, oy = (tx * (tx + 1) // 2) % 4, (tz * (tz + 1) // 2) % 4, (ty * (ty + 1) // 2) % 4
        oc = 1 - i % 2
        return (gx + ox) % 4, ((pz + oz) % 4) * 8 + ((py + oy) % 4) * 2 + (pc + oc) % 2

    barrier = pltpu.get_barrier_semaphore()

    def greet(i, carry):
        pl.semaphore_signal(barrier, inc=1, device_id=peer(i), device_id_type=MESH)
        return carry

    lax.fori_loop(0, DEV - 1, greet, 0)

    sub = lax.broadcasted_iota(jnp.int32, (128, 128), 0)
    lane = lax.broadcasted_iota(jnp.int32, (128, 128), 1)
    sub8 = lax.broadcasted_iota(jnp.int32, (8, 128), 0)

    def send(index):
        def one(i, carry):
            tx, ty = peer(i)
            pltpu.make_async_remote_copy(
                src_ref=snd.at[index, tx * 32 + ty], dst_ref=rcv.at[index, me],
                send_sem=snd_sem.at[index], recv_sem=rcv_sem.at[index],
                device_id=(tx, ty), device_id_type=MESH,
            ).start()
            return carry

        lax.fori_loop(0, DEV - 1, one, 0)
        rcv[index, pl.ds(me, 1), :] = snd[index, pl.ds(me, 1), :]

    def receive(index):
        rows = pl.ds(0, DEV - 1)
        pltpu.make_async_copy(
            snd.at[index, rows], rcv.at[index, rows], rcv_sem.at[index]
        ).wait()
        return rcv[index].T

    def sent(index):
        rows = pl.ds(0, DEV - 1)
        pltpu.make_async_copy(
            snd.at[index, rows], rcv.at[index, rows], snd_sem.at[index]
        ).wait()

    def post(index, dots=()):
        for j, value in enumerate(dots):
            mt[16 + j : 17 + j, :] = jnp.broadcast_to(value, (1, 128))
        snd[index] = mt[...].T
        send(index)

    def lane_sum(received, j):
        return jnp.sum(received[16 + j : 17 + j], axis=1, keepdims=True)

    mt[...] = jnp.zeros((128, 128), F32)
    pads[...] = jnp.zeros((2, 128, 128), jnp.int32)
    pads[0, :, 0:CAP] = cell_ref[0]
    pads[1, :, 0:CAP] = slot_ref[0]
    cells = pads[0].astype(F32).T[0:16].astype(jnp.int32)
    slots = pads[1].astype(F32).T[0:16].astype(jnp.int32)
    row_of = lax.shift_right_logical(cells, 7)
    col_of = lax.bitwise_and(cells, 127)
    well_of = lax.shift_right_logical(slots, 7)
    seg_of = lax.bitwise_and(slots, 127)
    for q in range(CAP):
        part = slice(q * 128, (q + 1) * 128)
        hot = jnp.where(sub == row_of[q : q + 1], 1.0, 0.0).astype(BF16)
        oht[0:128, part] = hot
        oht[128:256, part] = hot
        cmt[:, part] = jnp.where(sub == col_of[q : q + 1], 1.0, 0.0)
        seg_hot = jnp.where(sub == seg_of[q : q + 1], 1.0, 0.0)
        gt[:, part] = seg_hot.astype(BF16)
        gts[part, :] = seg_hot.T.astype(BF16)
        wmask[:, part] = jnp.where(sub8 == well_of[q : q + 1], 1.0, 0.0)
    vals[...] = jnp.zeros((48, 128), F32)
    for w in range(8):
        high, low = split(winv_ref[w].T)
        part = slice(w * 128, (w + 1) * 128)
        w2[0:128, part] = high.astype(BF16)
        w2[128:256, part] = low.astype(BF16)

    inner = lax.bitwise_and(sub, 15)
    layer = lax.shift_right_logical(sub, 4)
    outside = (
        (inner == 0) & (gx == 0),
        (inner == 15) & (gx == 3),
        (lane == 0) & (gy == 0),
        (lane == 127) & (gy == 31),
        layer == 0,
        layer == 7,
    )
    for n in range(6):
        faces[n] = jnp.where(outside[n], 0.0, flat(face_ref[n].astype(F32)))

    def gather(fields):
        stacked = jnp.concatenate([field.T for field in fields], axis=0)
        high, low = split(stacked)
        pair = jnp.concatenate([high.astype(BF16), low.astype(BF16)], axis=1)
        for q in range(0, CAP, 2):
            part = slice(q * 128, (q + 2) * 128)
            picked = dot(pair, oht[:, part])
            mask = cmt[:, part]
            for c in range(3):
                value = jnp.sum(picked[c * 128 : (c + 1) * 128] * mask, axis=0, keepdims=True)
                vals[c * 16 + q : c * 16 + q + 1, :] = value[:, 0:128]
                vals[c * 16 + q + 1 : c * 16 + q + 2, :] = value[:, 128:256]

    def by_slot(rows):
        high, low = split(rows)
        both = jnp.concatenate([high, low], axis=0).astype(BF16)
        spread = dot(both, gt[...])
        count = rows.shape[0]
        spread = spread[0:count] + spread[count:]
        return [
            jnp.sum(spread[n : n + 8] * wmask[...], axis=0, keepdims=True)
            for n in range(0, count, 8)
        ]

    def put_rows(ref, base, row):
        for q in range(CAP):
            ref[base + q : base + q + 1, :] = row[:, q * 128 : (q + 1) * 128]

    def solve_wells(rate):
        spread = jnp.concatenate(
            [jnp.broadcast_to(rate[q : q + 1], (8, 128)) for q in range(CAP)], axis=1
        ) * wmask[...]
        high, low = split(spread)
        totals = dot(jnp.concatenate([high, low], axis=0).astype(BF16), gts[...])
        high, low = split(totals[0:8] + totals[8:16])
        left = jnp.concatenate(
            [
                jnp.concatenate([high, high], axis=1),
                jnp.concatenate([low, jnp.zeros_like(low)], axis=1),
            ],
            axis=0,
        ).astype(BF16)
        product = dot(left, w2[...])
        product = product[0:8] + product[8:16]
        seg = jnp.zeros((8, 128), F32)
        for w in range(8):
            seg = jnp.where(sub8 == w, product[:, w * 128 : (w + 1) * 128], seg)
        put_rows(mt, 0, by_slot(seg)[0])

    def scatter(back):
        pieces = []
        for c in range(3):
            pieces.append(split(coef[3 + c] * back))
        stacked = []
        for half in range(2):
            for q in range(CAP):
                mask = cmt[:, q * 128 : (q + 1) * 128]
                stacked.append(
                    jnp.concatenate(
                        [mask * pieces[c][half][q : q + 1] for c in range(3)], axis=0
                    ).astype(BF16)
                )
        right = jnp.concatenate(stacked, axis=1)
        left = jnp.concatenate([oht[0:128], oht[0:128]], axis=1)
        term = dot_nt(left, right)
        return [term[:, c * 128 : (c + 1) * 128] for c in range(3)]

    def couple(ref, fields, a):
        out = flat(ref[:, a, 0].astype(F32)) * fields[0]
        out = out + flat(ref[:, a, 1].astype(F32)) * fields[1]
        return out + flat(ref[:, a, 2].astype(F32)) * fields[2]

    def halo_copies(op):
        low, high = (gx + 3) % 4, (gx + 1) % 4
        left, right = (gy + 31) % 32, (gy + 1) % 32

        def row_copy(mine, theirs, which, target):
            return pltpu.make_async_remote_copy(
                src_ref=flux_pad.at[op, :, :, mine], dst_ref=flux_pad.at[op, :, :, theirs],
                send_sem=hs_sem.at[op, which], recv_sem=hr_sem.at[op, which],
                device_id=(target, gy), device_id_type=MESH,
            )

        def col_copy(which, target):
            return pltpu.make_async_remote_copy(
                src_ref=col_snd.at[op], dst_ref=col_rcv.at[op, which],
                send_sem=hs_sem.at[op, 2 + which], recv_sem=hr_sem.at[op, 2 + which],
                device_id=(gx, target), device_id_type=MESH,
            )

        return (
            row_copy(23, 7, 0, high),
            row_copy(8, 24, 1, low),
            col_copy(0, right),
            col_copy(1, left),
        )

    def stencil_start(op, fields):
        fluxes = [couple(mob_ref, fields, a) for a in range(3)]
        packed = jnp.zeros((128, 128), F32)
        for a in range(3):
            flux_pad[op, a, :, 8:24, :] = fluxes[a].reshape(8, 16, 128)
            packed = jnp.where(lane == a, fluxes[a][:, 127:128], packed)
            packed = jnp.where(lane == 3 + a, fluxes[a][:, 0:1], packed)
        col_snd[op] = packed.T[0:8]
        copies = halo_copies(op)
        for copy in copies:
            copy.start()
        centre = []
        for a in range(3):
            flux = fluxes[a]
            zero = jnp.zeros((16, 128), F32)
            out = couple(diag_ref, fields, a)
            out = out - faces[4] * jnp.concatenate([zero, flux[0:112]], axis=0)
            out = out - faces[5] * jnp.concatenate([flux[16:128], zero], axis=0)
            centre.append(out)
        return copies, centre

    def stencil_end(op, copies, centre):
        for copy in copies:
            copy.wait()
        edge_low = jnp.concatenate([col_rcv[op, 0], jnp.zeros((120, 128), F32)], axis=0).T
        edge_high = jnp.concatenate([col_rcv[op, 1], jnp.zeros((120, 128), F32)], axis=0).T
        outs = []
        for a in range(3):
            flux = flat(flux_pad[op, a, :, 8:24, :])
            before = jnp.where(lane == 0, edge_low[:, a : a + 1], pltpu.roll(flux, 1, 1))
            after = jnp.where(lane == 127, edge_high[:, 3 + a : 4 + a], pltpu.roll(flux, 127, 1))
            out = centre[a] - faces[0] * flat(flux_pad[op, a, :, 7:23, :])
            out = out - faces[1] * flat(flux_pad[op, a, :, 9:25, :])
            out = out - faces[2] * before
            outs.append(out - faces[3] * after)
        return outs

    def precondition(fields):
        paired = [field.reshape(4, 2, 16, 128) for field in fields]
        results = []
        for e in range(6):
            total = None
            for f in range(6):
                term = colinv_ref[:, e, f].astype(F32) * paired[f % 3][:, f // 3]
                total = term if total is None else total + term
            results.append(total)
        return [
            flat(jnp.concatenate([results[c][:, None], results[3 + c][:, None]], axis=1))
            for c in range(3)
        ]

    def combine(scale, xs, ys):
        return [x + scale * y for x, y in zip(xs, ys)]

    guess = [flat(guess_ref[:, c]) for c in range(3)]
    gather(guess)
    mt[0:48, :] = vals[...]
    snd[0] = mt[...].T
    pl.semaphore_wait(barrier, DEV - 1)
    send(0)
    started = stencil_start(0, guess)
    rows = [win_ref[c : c + 1, w * 128 : (w + 1) * 128] for c in range(3) for w in range(8)]
    rows += [wout_ref[c : c + 1, w * 128 : (w + 1) * 128] for c in range(3) for w in range(8)]
    own = by_slot(jnp.concatenate(rows, axis=0))
    mt[...] = jnp.zeros((128, 128), F32)
    for n in range(6):
        put_rows(mt, 16 + n * 16, own[n])
    got = receive(0)
    rate = sum(mt[16 + 16 * c : 32 + 16 * c, :] * got[16 * c : 16 * c + 16] for c in range(3))
    solve_wells(rate)
    post(1)
    applied = stencil_end(0, *started)
    got = receive(1)
    for n in range(6):
        coef[n] = got[16 + 16 * n : 32 + 16 * n]
    term = scatter(got[0:16])
    r0 = [flat(right_ref[:, c]) - (applied[c] - term[c]) for c in range(3)]

    def operate(op, fields, dots, on_first=None):
        gather(fields)
        mt[0:16, :] = coef[0] * vals[0:16] + coef[1] * vals[16:32] + coef[2] * vals[32:48]
        post(2 * op, dots)
        started = stencil_start(op, fields)
        got = receive(2 * op)
        sums = [lane_sum(got, j) for j in range(len(dots))]
        solve_wells(got[0:16])
        extra = () if on_first is None else on_first(sums)
        post(2 * op + 1, extra)
        applied = stencil_end(op, *started)
        got = receive(2 * op + 1)
        late = [lane_sum(got, j) for j in range(len(extra))]
        term = scatter(got[0:16])
        return [applied[c] - term[c] for c in range(3)], sums, late

    u1 = precondition(r0)
    v0, (rho0,), _ = operate(1, u1, [local_sum(r0, r0)])
    u2 = precondition(v0)
    y0, (projected,), _ = operate(2, u2, [local_sum(r0, v0)])
    alpha0 = rho0 / projected
    s0 = combine(-alpha0, r0, v0)
    t0 = combine(-alpha0, v0, y0)
    u3 = precondition(t0)

    def new_rho(sums):
        r1 = combine(-(sums[0] / sums[1]), s0, t0)
        return [local_sum(r0, r1)]

    w0, (cross0, self0), (rho1,) = operate(
        3, u3, [local_sum(t0, s0), local_sum(t0, t0)], new_rho
    )
    omega0 = cross0 / self0
    beta = rho1 / rho0 * (alpha0 / omega0)
    r1 = combine(-omega0, s0, t0)
    a_r1 = combine(-omega0, t0, w0)
    v1 = combine(beta, a_r1, combine(-omega0, v0, y0))
    u4 = precondition(v1)
    y1, (projected1,), _ = operate(4, u4, [local_sum(r0, v1)])
    alpha1 = rho1 / projected1
    s1 = combine(-alpha1, r1, v1)
    t1 = combine(-alpha1, a_r1, y1)
    post(10, [local_sum(t1, s1), local_sum(t1, t1)])
    ms0 = combine(-alpha0, u1, u2)
    mr1 = combine(-omega0, ms0, u3)
    mp1 = combine(beta, mr1, combine(-omega0, u1, u2))
    ms1 = combine(-alpha1, mr1, u4)
    guess = [flat(guess_ref[:, c]) for c in range(3)]
    partial = combine(alpha1, combine(omega0, combine(alpha0, guess, u1), ms0), mp1)
    got = receive(10)
    omega1 = lane_sum(got, 0) / lane_sum(got, 1)
    final = combine(omega1, partial, ms1)
    left = combine(-omega1, s1, t1)
    for c in range(3):
        sol_ref[:, c] = final[c].reshape(8, 16, 128)
        res_ref[:, c] = left[c].reshape(8, 16, 128)
    for index in range(EXCHANGES):
        sent(index)


def per_device(*args):
    shape = args[0].shape
    vmem = pl.BlockSpec(memory_space=pltpu.VMEM)
    return pl.pallas_call(
        kernel,
        out_shape=(jax.ShapeDtypeStruct(shape, F32), jax.ShapeDtypeStruct(shape, F32)),
        in_specs=[vmem] * 11,
        out_specs=(vmem, vmem),
        scratch_shapes=[
            pltpu.VMEM((EXCHANGES, 128, 128), F32),
            pltpu.VMEM((EXCHANGES, 128, 128), F32),
            pltpu.VMEM((OPS, 3, 8, 32, 128), F32),
            pltpu.VMEM((OPS, 8, 128), F32),
            pltpu.VMEM((OPS, 2, 8, 128), F32),
            pltpu.VMEM((128, 128), F32),
            pltpu.VMEM((2, 128, 128), jnp.int32),
            pltpu.VMEM((6, 128, 128), F32),
            pltpu.VMEM((256, SLOTS), BF16),
            pltpu.VMEM((128, SLOTS), F32),
            pltpu.VMEM((SLOTS, 128), BF16),
            pltpu.VMEM((128, SLOTS), BF16),
            pltpu.VMEM((8, SLOTS), F32),
            pltpu.VMEM((256, 1024), BF16),
            pltpu.VMEM((48, 128), F32),
            pltpu.VMEM((6, 16, 128), F32),
            pltpu.SemaphoreType.DMA((EXCHANGES,)),
            pltpu.SemaphoreType.DMA((EXCHANGES,)),
            pltpu.SemaphoreType.DMA((OPS, 4)),
            pltpu.SemaphoreType.DMA((OPS, 4)),
        ],
        compiler_params=pltpu.CompilerParams(
            collective_id=0, has_side_effects=True, vmem_limit_bytes=48 * 1024 * 1024
        ),
    )(*args)


def solution(mesh):
    in_specs = (
        P(None, None, "gx", "gy"),
        P(None, None, "gx", "gy"),
        P(None, None, None, "gx", "gy"),
        P(None, None, None, "gx", "gy"),
        P(None, None, "gx", "gy"),
        P(None, None, None, "gx", "gy"),
        P(("gx", "gy"), None, None),
        P(("gx", "gy"), None, None),
        P(None, ("gx", "gy")),
        P(None, ("gx", "gy")),
        P(("gx", "gy"), None, None),
    )
    out_specs = (P(None, None, "gx", "gy"), P(None, None, "gx", "gy"))
    return jax.shard_map(
        per_device, mesh=mesh, in_specs=in_specs, out_specs=out_specs, check_vma=False
    )
```

time: 1000 us -> 156 us (0.16)
  blocking collectives: 315 us -> 0 us
  local copies, waits for them, and re-layouts: 258 us -> 9.69 us
  other arithmetic: 167 us -> 0 us
  starting transfers between devices: 161 us -> 0 us
  Pallas kernels: 0 us -> 145 us
  waiting for transfers between devices: 71.8 us -> 0 us
  between operations: 12.6 us -> 0.67 us
    psum x5 -> x0, blocking collectives: 315 us -> none  [the longest x2 126 us: per_device(): lax.psum((jnp.sum(response * halfway), jnp.sum(response * response)), ('g...]
    pallas_call x0 -> x1, Pallas kernels: none -> 145 us  [per_device(): pl.pallas_call(kernel, out_shape=(jax.ShapeDtypeStruct(shape, F32), jax.S...]
    gather x36 -> x0, local copies, waits for them, and re-layouts: 129 us -> none  [the longest x18 74.6 us: well_term(): values = flattened[layer_idx, :, column_idx]]
    all_to_all x12 -> x0, starting transfers between devices: 94.1 us -> none  [the longest x6 54 us: well_term(): lax.all_to_all(pad_out[:, targets] * back[None], ('gx', 'gy'), split_axis...]
    unnamed x9 -> x0, other arithmetic: 78.4 us -> none
    all_to_all x12 -> x0, waiting for transfers between devices: 71.7 us -> none  [the longest x6 54.3 us: well_term(): lax.all_to_all(pad_out[:, targets] * back[None], ('gx', 'gy'), split_axis...]
    ppermute x24 -> x0, starting transfers between devices: 66.6 us -> none  [the longest x12 39.9 us: padded_2(): lax.ppermute(lax.slice_in_dim(block, block.shape[dim] - width, None, axis...]
    scatter-add x6 -> x0, other arithmetic: 44.5 us -> none  [solve_wells(): totals = jnp.zeros((per_owner + 1,), jnp.float32).at[targets].add(rate)]
  transfers between devices with their start and end apart: 36 -> 0, of which waited for: 11 -> 0; matrix products, arithmetic and copies ran while one was open for 38% -> 0% of each run, Pallas kernels for 0% -> 0%
where the time goes in v1:
time: 156 us
  Pallas kernels  145 us (93%)
  local copies, waits for them, and re-layouts  9.69 us (6%)
    pallas_call x1, Pallas kernels, per_device(): pl.pallas_call(kernel, out_shape=(jax.ShapeDtypeStruct(shape, F32), jax.S...  145 us
    unnamed x24, local copies, waits for them, and re-layouts  9.69 us

profile of v1, /device:TPU:1, one launch (start us, length us, event | category | flops | bytes accessed | tf_op | source)
XLA Modules:
  0.0 155.8 jit_solution(8181280084647009833)
XLA Ops:
  0.6 0.0 copy-start.9
  0.6 0.8 copy.13.cell_ref
  1.4 0.0 copy-done.9
  1.4 0.0 copy-start.7
  1.5 0.0 copy-start.8
  1.5 0.1 copy.14.slot_ref
  1.6 0.6 copy-done.7
  2.2 0.0 copy-done.8
  2.2 0.0 copy-start
  2.2 1.1 copy-done
  3.2 0.0 copy-start.1
  3.2 1.0 copy-done.1
  4.3 0.0 copy-start.2
  4.3 1.0 copy-done.2
  5.3 0.0 copy-start.3
  5.3 1.0 copy-done.3
  6.2 0.0 copy-start.4
  6.2 0.9 copy-done.4
  7.1 0.0 copy-start.5
  7.1 0.9 copy-done.5
  8.1 0.9 copy-done.6
  9.0 145.5 %shard_map.122 = (f32[8,3,16,128]{3,2,1,0:T(8,128)S(1)}, f32[8,3,16,128]{3,2,1,0:T(8,128)S(1)}) custom-call(f32[8,3,16,128]{3,2,1,0:T(8,128)S(1)} %copy-done.4, f32[8,3,16,128]{3,2,1,0:T(8,128)S(1)} %copy-done.5, bf16[8,3,3,16,128]{4,3,2,1,0:T(8,128)(2,1)S(1)} %copy-done.2, bf16[8,3,3,16,128]{4,3,2,1,0:T(8,128)(2,1)S(1)} %copy-done.3, ...), custom_call_target="tpu_custom_call" | custom-call | tf_op jit(solution)/shard_map/pallas_call | solution.py:382
  154.5 0.7 copy.17
  155.1 0.7 copy.18
  (1 shorter events, 0.0 us)
Async XLA Ops:
  0.6 0.8 copy-start.9
  1.4 0.7 copy-start.7
  1.5 0.7 copy-start.8
  2.2 1.1 copy-start
  3.2 1.0 copy-start.1
  4.3 1.0 copy-start.2
  5.3 1.0 copy-start.3
  6.2 0.9 copy-start.4
  7.1 0.9 copy-start.5
  8.1 0.9 copy-start.6

commit v2 on v1

--- a/solution.py
+++ b/solution.py
@@ -10,6 +10,7 @@
 BF16 = jnp.bfloat16
 DEV = 128
 CAP = 10
+FAR_FIRST = (2, 3, 1, 0)
 SLOTS = DEV * CAP
 OPS = 5
 EXCHANGES = 2 * OPS + 1
@@ -38,45 +39,64 @@
 
 
 def kernel(
+    right_in, guess_in, diag_in, mob_in, face_in, colinv_in, cell_in, slot_in, win_in, wout_in,
+    winv_in, sol_ref, res_ref,
     right_ref, guess_ref, diag_ref, mob_ref, face_ref, colinv_ref, cell_ref, slot_ref, win_ref,
-    wout_ref, winv_ref, sol_ref, res_ref,
-    snd, rcv, flux_pad, col_snd, col_rcv, mt, pads, faces, oht, cmt, gts, gt, wmask, w2, vals, coef,
+    wout_ref, winv_ref, load_sem,
+    snd, rcv, flux_pad, col_snd, col_rcv, mt, faces, oht, cmt, gts, gt, wmask, w2, vals, coef,
     snd_sem, rcv_sem, hs_sem, hr_sem,
 ):
     gx = lax.axis_index("gx")
     gy = lax.axis_index("gy")
     me = gx * 32 + gy
-    pz, py, pc = gy // 8, (gy // 2) % 4, gy % 2
-
-    def peer(i):
-        tx, tz, ty = 3 - i // 32, 3 - (i // 8) % 4, 3 - (i // 2) % 4
-        ox, oz, oy = (tx * (tx + 1) // 2) % 4, (tz * (tz + 1) // 2) % 4, (ty * (ty + 1) // 2) % 4
-        oc = 1 - i % 2
-        return (gx + ox) % 4, ((pz + oz) % 4) * 8 + ((py + oy) % 4) * 2 + (pc + oc) % 2
+    pz, py, pc = lax.div(gy, 8), lax.rem(lax.div(gy, 2), 4), lax.rem(gy, 2)
+    near = [
+        (oy, oc, lax.rem(py + oy, 4) * 2 + (1 - pc if oc else pc)) for oy in FAR_FIRST for oc in (1, 0)
+    ]
+
+    def every_peer(act):
+        def some(i, carry):
+            tx, tz = 3 - lax.div(i, 4), 3 - lax.rem(i, 4)
+            dx = lax.rem(gx + lax.div(tx * (tx + 1), 2), 4)
+            dz = lax.rem(pz + lax.div(tz * (tz + 1), 2), 4) * 8
+            for _, _, low in near:
+                act(dx, dz + low)
+            return carry
+
+        lax.fori_loop(0, 15, some, 0)
+        for oy, oc, low in near:
+            if oy or oc:
+                act(gx, pz * 8 + low)
 
     barrier = pltpu.get_barrier_semaphore()
 
-    def greet(i, carry):
-        pl.semaphore_signal(barrier, inc=1, device_id=peer(i), device_id_type=MESH)
-        return carry
-
-    lax.fori_loop(0, DEV - 1, greet, 0)
+    def greet(tx, ty):
+        pl.semaphore_signal(barrier, inc=1, device_id=(tx, ty), device_id_type=MESH)
+
+    every_peer(greet)
+    loads = {}
+    for n, (name, src, dst) in enumerate((
+        ("cell", cell_in, cell_ref), ("guess", guess_in, guess_ref), ("slot", slot_in, slot_ref),
+        ("winv", winv_in, winv_ref), ("face", face_in, face_ref), ("win", win_in, win_ref),
+        ("wout", wout_in, wout_ref), ("mob", mob_in, mob_ref), ("diag", diag_in, diag_ref),
+        ("right", right_in, right_ref), ("colinv", colinv_in, colinv_ref),
+    )):
+        loads[name] = pltpu.make_async_copy(src, dst, load_sem.at[n])
+        loads[name].start()
 
     sub = lax.broadcasted_iota(jnp.int32, (128, 128), 0)
     lane = lax.broadcasted_iota(jnp.int32, (128, 128), 1)
     sub8 = lax.broadcasted_iota(jnp.int32, (8, 128), 0)
 
     def send(index):
-        def one(i, carry):
-            tx, ty = peer(i)
+        def one(tx, ty):
             pltpu.make_async_remote_copy(
                 src_ref=snd.at[index, tx * 32 + ty], dst_ref=rcv.at[index, me],
                 send_sem=snd_sem.at[index], recv_sem=rcv_sem.at[index],
                 device_id=(tx, ty), device_id_type=MESH,
             ).start()
-            return carry
-
-        lax.fori_loop(0, DEV - 1, one, 0)
+
+        every_peer(one)
         rcv[index, pl.ds(me, 1), :] = snd[index, pl.ds(me, 1), :]
 
     def receive(index):
@@ -102,26 +122,28 @@
         return jnp.sum(received[16 + j : 17 + j], axis=1, keepdims=True)
 
     mt[...] = jnp.zeros((128, 128), F32)
-    pads[...] = jnp.zeros((2, 128, 128), jnp.int32)
-    pads[0, :, 0:CAP] = cell_ref[0]
-    pads[1, :, 0:CAP] = slot_ref[0]
-    cells = pads[0].astype(F32).T[0:16].astype(jnp.int32)
-    slots = pads[1].astype(F32).T[0:16].astype(jnp.int32)
+    loads["cell"].wait()
+    cells = cell_ref[:, 0, :]
     row_of = lax.shift_right_logical(cells, 7)
     col_of = lax.bitwise_and(cells, 127)
-    well_of = lax.shift_right_logical(slots, 7)
-    seg_of = lax.bitwise_and(slots, 127)
     for q in range(CAP):
         part = slice(q * 128, (q + 1) * 128)
         hot = jnp.where(sub == row_of[q : q + 1], 1.0, 0.0).astype(BF16)
         oht[0:128, part] = hot
         oht[128:256, part] = hot
         cmt[:, part] = jnp.where(sub == col_of[q : q + 1], 1.0, 0.0)
+    vals[...] = jnp.zeros((48, 128), F32)
+    loads["slot"].wait()
+    slots = slot_ref[:, 0, :]
+    well_of = lax.shift_right_logical(slots, 7)
+    seg_of = lax.bitwise_and(slots, 127)
+    for q in range(CAP):
+        part = slice(q * 128, (q + 1) * 128)
         seg_hot = jnp.where(sub == seg_of[q : q + 1], 1.0, 0.0)
         gt[:, part] = seg_hot.astype(BF16)
         gts[part, :] = seg_hot.T.astype(BF16)
         wmask[:, part] = jnp.where(sub8 == well_of[q : q + 1], 1.0, 0.0)
-    vals[...] = jnp.zeros((48, 128), F32)
+    loads["winv"].wait()
     for w in range(8):
         high, low = split(winv_ref[w].T)
         part = slice(w * 128, (w + 1) * 128)
@@ -138,6 +160,7 @@
         layer == 0,
         layer == 7,
     )
+    loads["face"].wait()
     for n in range(6):
         faces[n] = jnp.where(outside[n], 0.0, flat(face_ref[n].astype(F32)))
 
@@ -292,10 +315,13 @@
     def combine(scale, xs, ys):
         return [x + scale * y for x, y in zip(xs, ys)]
 
+    loads["guess"].wait()
     guess = [flat(guess_ref[:, c]) for c in range(3)]
     gather(guess)
     mt[0:48, :] = vals[...]
     snd[0] = mt[...].T
+    for name in ("win", "wout", "mob", "diag", "right", "colinv"):
+        loads[name].wait()
     pl.semaphore_wait(barrier, DEV - 1)
     send(0)
     started = stencil_start(0, guess)
@@ -377,21 +403,26 @@
 
 
 def per_device(*args):
+    args = list(args)
+    for n in (6, 7):
+        args[n] = jnp.transpose(args[n], (2, 0, 1))
     shape = args[0].shape
+    hbm = pl.BlockSpec(memory_space=pltpu.HBM)
     vmem = pl.BlockSpec(memory_space=pltpu.VMEM)
     return pl.pallas_call(
         kernel,
         out_shape=(jax.ShapeDtypeStruct(shape, F32), jax.ShapeDtypeStruct(shape, F32)),
-        in_specs=[vmem] * 11,
+        in_specs=[hbm] * 11,
         out_specs=(vmem, vmem),
-        scratch_shapes=[
+        scratch_shapes=[pltpu.VMEM(arg.shape, arg.dtype) for arg in args]
+        + [
+            pltpu.SemaphoreType.DMA((11,)),
             pltpu.VMEM((EXCHANGES, 128, 128), F32),
             pltpu.VMEM((EXCHANGES, 128, 128), F32),
             pltpu.VMEM((OPS, 3, 8, 32, 128), F32),
             pltpu.VMEM((OPS, 8, 128), F32),
             pltpu.VMEM((OPS, 2, 8, 128), F32),
             pltpu.VMEM((128, 128), F32),
-            pltpu.VMEM((2, 128, 128), jnp.int32),
             pltpu.VMEM((6, 128, 128), F32),
             pltpu.VMEM((256, SLOTS), BF16),
             pltpu.VMEM((128, SLOTS), F32),
@@ -407,7 +438,7 @@
             pltpu.SemaphoreType.DMA((OPS, 4)),
         ],
         compiler_params=pltpu.CompilerParams(
-            collective_id=0, has_side_effects=True, vmem_limit_bytes=48 * 1024 * 1024
+            collective_id=0, has_side_effects=True, vmem_limit_bytes=60 * 1024 * 1024
         ),
     )(*args)
 

time: 156 us -> 91.1 us (0.58)
  Pallas kernels: 145 us -> 88 us
  local copies, waits for them, and re-layouts: 9.69 us -> 2.34 us
    pallas_call x1, Pallas kernels: 145 us -> 88 us  [per_device(): pl.pallas_call(kernel, out_shape=(jax.ShapeDtypeStruct(shape, F32), jax.S...]
    unnamed x24 -> x4, local copies, waits for them, and re-layouts: 9.69 us -> 2.34 us
where the time goes in v2:
time: 91.1 us; the launch traced here: 91 us
  Pallas kernels  88 us (97%)
  local copies, waits for them, and re-layouts  2.34 us (3%)
    pallas_call x1, Pallas kernels, per_device(): pl.pallas_call(kernel, out_shape=(jax.ShapeDtypeStruct(shape, F32), jax.S...  88 us
    unnamed x4, local copies, waits for them, and re-layouts  2.34 us

profile of v2, /device:TPU:1, one launch (start us, length us, event | category | flops | bytes accessed | tf_op | source)
XLA Modules:
  0.0 91.0 jit_solution(7754047828129852740)
XLA Ops:
  0.6 88.0 %shard_map.122 = (f32[8,3,16,128]{3,2,1,0:T(8,128)}, f32[8,3,16,128]{3,2,1,0:T(8,128)}) custom-call(f32[8,3,16,128]{3,2,1,0:T(8,128)} %right_in.1, f32[8,3,16,128]{3,2,1,0:T(8,128)} %guess_in.1, bf16[8,3,3,16,128]{4,3,2,1,0:T(8,128)(2,1)} %diag_in.1, bf16[8,3,3,16,128]{4,3,2,1,0:T(8,128)(2,1)} %mob_in.1, bf16[6,8,16,128]{3,2,1,0:T(8,128)(2,1)} %face_in.1, ...), custom_call_target="tpu_custom_call" | custom-call | tf_op jit(solution)/shard_map/pallas_call | solution.py:412
  88.6 0.0 copy-start
  88.6 1.7 %copy.15 = f32[8,3,16,128]{3,2,1,0:T(8,128)} copy(f32[8,3,16,128]{3,2,1,0:T(8,128)} %get-tuple-element.4) | data formatting | bytes 393216
  90.3 0.0 copy-done
  90.3 0.7 copy.16
Async XLA Ops:
  88.6 1.7 %copy-start = (f32[8,3,16,128]{3,2,1,0:T(8,128)S(1)}, f32[8,3,16,128]{3,2,1,0:T(8,128)}, u32[]{:S(2)}) copy-start(f32[8,3,16,128]{3,2,1,0:T(8,128)} %get-tuple-element.5) | copy-start | bytes 589828

commit v3 on v2

--- a/solution.py
+++ b/solution.py
@@ -43,7 +43,8 @@
     winv_in, sol_ref, res_ref,
     right_ref, guess_ref, diag_ref, mob_ref, face_ref, colinv_ref, cell_ref, slot_ref, win_ref,
     wout_ref, winv_ref, load_sem,
-    snd, rcv, flux_pad, col_snd, col_rcv, mt, faces, oht, cmt, gts, gt, wmask, w2, vals, coef,
+    snd, rcv, flux_pad, col_snd, col_rcv, mt, faces, oht, cmt, cmb, terms, gts, gt, wmask, solver, vals, coef, link,
+    link_w, link_a, link_out,
     snd_sem, rcv_sem, hs_sem, hr_sem,
 ):
     gx = lax.axis_index("gx")
@@ -54,19 +55,15 @@
         (oy, oc, lax.rem(py + oy, 4) * 2 + (1 - pc if oc else pc)) for oy in FAR_FIRST for oc in (1, 0)
     ]
 
+    xs = [lax.rem(gx + o, 4) for o in range(4)]
+    zs = [lax.rem(pz + o, 4) * 8 for o in range(4)]
+
     def every_peer(act):
-        def some(i, carry):
-            tx, tz = 3 - lax.div(i, 4), 3 - lax.rem(i, 4)
-            dx = lax.rem(gx + lax.div(tx * (tx + 1), 2), 4)
-            dz = lax.rem(pz + lax.div(tz * (tz + 1), 2), 4) * 8
-            for _, _, low in near:
-                act(dx, dz + low)
-            return carry
-
-        lax.fori_loop(0, 15, some, 0)
-        for oy, oc, low in near:
-            if oy or oc:
-                act(gx, pz * 8 + low)
+        for ox in FAR_FIRST:
+            for oz in FAR_FIRST:
+                for oy, oc, low in near:
+                    if ox or oz or oy or oc:
+                        act(xs[ox], zs[oz] + low)
 
     barrier = pltpu.get_barrier_semaphore()
 
@@ -131,39 +128,10 @@
         hot = jnp.where(sub == row_of[q : q + 1], 1.0, 0.0).astype(BF16)
         oht[0:128, part] = hot
         oht[128:256, part] = hot
-        cmt[:, part] = jnp.where(sub == col_of[q : q + 1], 1.0, 0.0)
+        col_hot = jnp.where(sub == col_of[q : q + 1], 1.0, 0.0)
+        cmt[:, part] = col_hot
+        cmb[:, part] = col_hot.astype(BF16)
     vals[...] = jnp.zeros((48, 128), F32)
-    loads["slot"].wait()
-    slots = slot_ref[:, 0, :]
-    well_of = lax.shift_right_logical(slots, 7)
-    seg_of = lax.bitwise_and(slots, 127)
-    for q in range(CAP):
-        part = slice(q * 128, (q + 1) * 128)
-        seg_hot = jnp.where(sub == seg_of[q : q + 1], 1.0, 0.0)
-        gt[:, part] = seg_hot.astype(BF16)
-        gts[part, :] = seg_hot.T.astype(BF16)
-        wmask[:, part] = jnp.where(sub8 == well_of[q : q + 1], 1.0, 0.0)
-    loads["winv"].wait()
-    for w in range(8):
-        high, low = split(winv_ref[w].T)
-        part = slice(w * 128, (w + 1) * 128)
-        w2[0:128, part] = high.astype(BF16)
-        w2[128:256, part] = low.astype(BF16)
-
-    inner = lax.bitwise_and(sub, 15)
-    layer = lax.shift_right_logical(sub, 4)
-    outside = (
-        (inner == 0) & (gx == 0),
-        (inner == 15) & (gx == 3),
-        (lane == 0) & (gy == 0),
-        (lane == 127) & (gy == 31),
-        layer == 0,
-        layer == 7,
-    )
-    loads["face"].wait()
-    for n in range(6):
-        faces[n] = jnp.where(outside[n], 0.0, flat(face_ref[n].astype(F32)))
-
     def gather(fields):
         stacked = jnp.concatenate([field.T for field in fields], axis=0)
         high, low = split(stacked)
@@ -206,27 +174,21 @@
             ],
             axis=0,
         ).astype(BF16)
-        product = dot(left, w2[...])
-        product = product[0:8] + product[8:16]
-        seg = jnp.zeros((8, 128), F32)
-        for w in range(8):
-            seg = jnp.where(sub8 == w, product[:, w * 128 : (w + 1) * 128], seg)
-        put_rows(mt, 0, by_slot(seg)[0])
+        product = dot(left, solver[...])
+        product = (product[0:8] + product[8:16]) * wmask[...]
+        put_rows(mt, 0, jnp.sum(product, axis=0, keepdims=True))
 
     def scatter(back):
-        pieces = []
-        for c in range(3):
-            pieces.append(split(coef[3 + c] * back))
-        stacked = []
+        pieces = [split(coef[3 + c] * back) for c in range(3)]
         for half in range(2):
             for q in range(CAP):
-                mask = cmt[:, q * 128 : (q + 1) * 128]
-                stacked.append(
-                    jnp.concatenate(
-                        [mask * pieces[c][half][q : q + 1] for c in range(3)], axis=0
-                    ).astype(BF16)
-                )
-        right = jnp.concatenate(stacked, axis=1)
+                part = slice(q * 128, (q + 1) * 128)
+                into = slice((half * CAP + q) * 128, (half * CAP + q + 1) * 128)
+                for c in range(3):
+                    row = jnp.broadcast_to(pieces[c][half][q : q + 1], (16, 128)).astype(BF16)
+                    spread = jnp.concatenate([row] * 8, axis=0)
+                    terms[c * 128 : (c + 1) * 128, into] = cmb[:, part] * spread
+        right = terms[...]
         left = jnp.concatenate([oht[0:128], oht[0:128]], axis=1)
         term = dot_nt(left, right)
         return [term[:, c * 128 : (c + 1) * 128] for c in range(3)]
@@ -320,11 +282,46 @@
     gather(guess)
     mt[0:48, :] = vals[...]
     snd[0] = mt[...].T
+    pl.semaphore_wait(barrier, DEV - 1)
+    send(0)
     for name in ("win", "wout", "mob", "diag", "right", "colinv"):
         loads[name].wait()
-    pl.semaphore_wait(barrier, DEV - 1)
-    send(0)
+    inner = lax.bitwise_and(sub, 15)
+    layer = lax.shift_right_logical(sub, 4)
+    outside = (
+        (inner == 0) & (gx == 0),
+        (inner == 15) & (gx == 3),
+        (lane == 0) & (gy == 0),
+        (lane == 127) & (gy == 31),
+        layer == 0,
+        layer == 7,
+    )
+    loads["face"].wait()
+    for n in range(6):
+        faces[n] = jnp.where(outside[n], 0.0, flat(face_ref[n].astype(F32)))
+
     started = stencil_start(0, guess)
+    loads["slot"].wait()
+    slots = slot_ref[:, 0, :]
+    well_of = lax.shift_right_logical(slots, 7)
+    seg_of = lax.bitwise_and(slots, 127)
+    for q in range(CAP):
+        part = slice(q * 128, (q + 1) * 128)
+        seg_hot = jnp.where(sub == seg_of[q : q + 1], 1.0, 0.0)
+        gt[:, part] = seg_hot.astype(BF16)
+        gts[part, :] = seg_hot.T.astype(BF16)
+        wmask[:, part] = jnp.where(sub8 == well_of[q : q + 1], 1.0, 0.0)
+    loads["winv"].wait()
+    fused = None
+    for w in range(8):
+        high, low = split(winv_ref[w].T)
+        rows = dot(high.astype(BF16), gt[...]) + dot(low.astype(BF16), gt[...])
+        rows = rows * wmask[w : w + 1, :]
+        fused = rows if fused is None else fused + rows
+    high, low = split(fused)
+    solver[0:128, :] = high.astype(BF16)
+    solver[128:256, :] = low.astype(BF16)
+
     rows = [win_ref[c : c + 1, w * 128 : (w + 1) * 128] for c in range(3) for w in range(8)]
     rows += [wout_ref[c : c + 1, w * 128 : (w + 1) * 128] for c in range(3) for w in range(8)]
     own = by_slot(jnp.concatenate(rows, axis=0))
@@ -342,48 +339,145 @@
     term = scatter(got[0:16])
     r0 = [flat(right_ref[:, c]) - (applied[c] - term[c]) for c in range(3)]
 
-    def operate(op, fields, dots, on_first=None):
+    def rates_of(fields):
         gather(fields)
-        mt[0:16, :] = coef[0] * vals[0:16] + coef[1] * vals[16:32] + coef[2] * vals[32:48]
-        post(2 * op, dots)
-        started = stencil_start(op, fields)
-        got = receive(2 * op)
-        sums = [lane_sum(got, j) for j in range(len(dots))]
-        solve_wells(got[0:16])
-        extra = () if on_first is None else on_first(sums)
-        post(2 * op + 1, extra)
-        applied = stencil_end(op, *started)
-        got = receive(2 * op + 1)
-        late = [lane_sum(got, j) for j in range(len(extra))]
-        term = scatter(got[0:16])
-        return [applied[c] - term[c] for c in range(3)], sums, late
-
+        return coef[0] * vals[0:16] + coef[1] * vals[16:32] + coef[2] * vals[32:48]
+
+    def build_link():
+        half = lax.bitwise_and(lax.shift_right_logical(row_of, 4), 1)
+        key = lax.bitwise_and(row_of, 15) * 128 + col_of
+        key = (key + lax.shift_right_logical(row_of, 5) * 2048).astype(F32)
+        weights = []
+        for f in range(6):
+            stacked = jnp.concatenate(
+                [
+                    jnp.concatenate(
+                        [colinv_ref[:, c, f][:, None], colinv_ref[:, 3 + c, f][:, None]], axis=1
+                    ).astype(F32).reshape(128, 128).T
+                    for c in range(3)
+                ],
+                axis=0,
+            ).astype(BF16)
+            for q in range(0, CAP, 2):
+                part = slice(q * 128, (q + 2) * 128)
+                picked = dot(stacked, oht[0:128, part])
+                total = None
+                for c in range(3):
+                    row = jnp.concatenate(
+                        [coef[c, q : q + 1, :], coef[c, q + 1 : q + 2, :]], axis=1
+                    )
+                    term = picked[c * 128 : (c + 1) * 128] * row
+                    total = term if total is None else total + term
+                total = jnp.sum(total * cmt[:, part], axis=0, keepdims=True)
+                high, low = split(total)
+                link_w[f : f + 1, part] = high
+                link_w[6 + f : 7 + f, part] = high
+                link_w[12 + f : 13 + f, part] = low
+        link_w[18:32, :] = jnp.zeros((14, SLOTS), F32)
+        right = link_w[...].astype(BF16)
+        keys = jnp.concatenate([key[q : q + 1] for q in range(CAP)], axis=1)
+        link_a[...] = jnp.zeros((128, 128), F32)
+        for q in range(CAP):
+            for f in range(6):
+                own = jnp.where(half[q : q + 1] == f // 3, coef[3 + f % 3, q : q + 1, :], 0.0)
+                high, low = split(own)
+                link_a[f : f + 1, :] = high
+                link_a[6 + f : 7 + f, :] = low
+                link_a[12 + f : 13 + f, :] = high
+            link_a[32:33, :] = key[q : q + 1]
+            turned = link_a[...].T
+            product = dot(turned[:, 0:32].astype(BF16), right)
+            same = jnp.broadcast_to(turned[:, 32:33], (128, SLOTS)) == keys
+            link[q * 128 : (q + 1) * 128, :] = jnp.where(same, product, 0.0)
+
+    def linked(index):
+        total = jnp.zeros((8, SLOTS), F32)
+        for q in range(CAP):
+            for n in range(0, 128, 8):
+                value = jnp.broadcast_to(rcv[index, n : n + 8, q : q + 1], (8, SLOTS))
+                total = total + value * link[q * 128 + n : q * 128 + n + 8, :]
+        put_rows(link_out, 0, jnp.sum(total, axis=0, keepdims=True))
+        return link_out[...]
+
+    def compact_sum(left, right):
+        total = jnp.sum(left * right, axis=0, keepdims=True)
+        return jnp.sum(total, axis=1, keepdims=True)
+
+    def minus_wells(applied, back):
+        term = scatter(back)
+        return [applied[c] - term[c] for c in range(3)]
+
+    link_out[...] = jnp.zeros((16, 128), F32)
     u1 = precondition(r0)
-    v0, (rho0,), _ = operate(1, u1, [local_sum(r0, r0)])
+    mt[0:16, :] = rates_of(u1)
+    post(2)
+    started = stencil_start(1, u1)
+    build_link()
+    gather(r0)
+    r0_out = coef[3] * vals[0:16] + coef[4] * vals[16:32] + coef[5] * vals[32:48]
+    own_rho = local_sum(r0, r0)
+    solve_wells(receive(2)[0:16])
+    post(3, [own_rho])
+    d1 = stencil_end(1, *started)
+    rates_d = rates_of(precondition(d1))
+    own_d = local_sum(r0, d1)
+    got = receive(3)
+    rho0 = lane_sum(got, 0)
+    back = got[0:16]
+    rates2 = rates_d - linked(3)
+    own_v = own_d - compact_sum(r0_out, back)
+    mt[0:16, :] = rates2
+    post(4, [own_v])
+    v0 = minus_wells(d1, back)
     u2 = precondition(v0)
-    y0, (projected,), _ = operate(2, u2, [local_sum(r0, v0)])
-    alpha0 = rho0 / projected
+    started = stencil_start(2, u2)
+    got = receive(4)
+    alpha0 = rho0 / lane_sum(got, 0)
+    solve_wells(got[0:16])
+    post(5)
+    d2 = stencil_end(2, *started)
+    rates_d = rates_of(precondition(d2))
+    got = receive(5)
+    rates_y = rates_d - linked(5)
+    rates3 = rates2 - alpha0 * rates_y
+    mt[0:16, :] = rates3
+    post(6)
+    y0 = minus_wells(d2, got[0:16])
     s0 = combine(-alpha0, r0, v0)
     t0 = combine(-alpha0, v0, y0)
     u3 = precondition(t0)
-
-    def new_rho(sums):
-        r1 = combine(-(sums[0] / sums[1]), s0, t0)
-        return [local_sum(r0, r1)]
-
-    w0, (cross0, self0), (rho1,) = operate(
-        3, u3, [local_sum(t0, s0), local_sum(t0, t0)], new_rho
-    )
-    omega0 = cross0 / self0
+    started = stencil_start(3, u3)
+    own_y = local_sum(r0, y0)
+    own_t = local_sum(r0, t0)
+    own_dots = [local_sum(t0, s0), local_sum(t0, t0), local_sum(r0, s0), own_t]
+    solve_wells(receive(6)[0:16])
+    post(7, own_dots)
+    d3 = stencil_end(3, *started)
+    rates_d = rates_of(precondition(d3))
+    own_d = local_sum(r0, d3)
+    got = receive(7)
+    omega0 = lane_sum(got, 0) / lane_sum(got, 1)
+    rho1 = lane_sum(got, 2) - omega0 * lane_sum(got, 3)
     beta = rho1 / rho0 * (alpha0 / omega0)
+    back = got[0:16]
+    rates_w = rates_d - linked(7)
+    mt[0:16, :] = rates3 - omega0 * rates_w + beta * (rates2 - omega0 * rates_y)
+    own_w = own_d - compact_sum(r0_out, back)
+    post(8, [own_t - omega0 * own_w + beta * (own_v - omega0 * own_y)])
+    w0 = minus_wells(d3, back)
     r1 = combine(-omega0, s0, t0)
     a_r1 = combine(-omega0, t0, w0)
     v1 = combine(beta, a_r1, combine(-omega0, v0, y0))
     u4 = precondition(v1)
-    y1, (projected1,), _ = operate(4, u4, [local_sum(r0, v1)])
-    alpha1 = rho1 / projected1
+    started = stencil_start(4, u4)
+    got = receive(8)
+    alpha1 = rho1 / lane_sum(got, 0)
+    solve_wells(got[0:16])
+    post(9)
+    d4 = stencil_end(4, *started)
     s1 = combine(-alpha1, r1, v1)
-    t1 = combine(-alpha1, a_r1, y1)
+    got = receive(9)
+    t1 = combine(-alpha1, a_r1, minus_wells(d4, got[0:16]))
     post(10, [local_sum(t1, s1), local_sum(t1, t1)])
     ms0 = combine(-alpha0, u1, u2)
     mr1 = combine(-omega0, ms0, u3)
@@ -426,12 +520,18 @@
             pltpu.VMEM((6, 128, 128), F32),
             pltpu.VMEM((256, SLOTS), BF16),
             pltpu.VMEM((128, SLOTS), F32),
+            pltpu.VMEM((128, SLOTS), BF16),
+            pltpu.VMEM((384, 2 * SLOTS), BF16),
             pltpu.VMEM((SLOTS, 128), BF16),
             pltpu.VMEM((128, SLOTS), BF16),
             pltpu.VMEM((8, SLOTS), F32),
-            pltpu.VMEM((256, 1024), BF16),
+            pltpu.VMEM((256, SLOTS), BF16),
             pltpu.VMEM((48, 128), F32),
             pltpu.VMEM((6, 16, 128), F32),
+            pltpu.VMEM((SLOTS, SLOTS), F32),
+            pltpu.VMEM((32, SLOTS), F32),
+            pltpu.VMEM((128, 128), F32),
+            pltpu.VMEM((16, 128), F32),
             pltpu.SemaphoreType.DMA((EXCHANGES,)),
             pltpu.SemaphoreType.DMA((EXCHANGES,)),
             pltpu.SemaphoreType.DMA((OPS, 4)),

time: 91.1 us -> 87 us (0.955)
  Pallas kernels: 88 us -> 83.8 us
    pallas_call x1, Pallas kernels: 88 us -> 83.8 us  [per_device(): pl.pallas_call(kernel, out_shape=(jax.ShapeDtypeStruct(shape, F32), jax.S...]
where the time goes in v3:
time: 87 us; the launch traced here: 86.8 us
  Pallas kernels  83.8 us (96%)
  local copies, waits for them, and re-layouts  2.34 us (3%)
    pallas_call x1, Pallas kernels, per_device(): pl.pallas_call(kernel, out_shape=(jax.ShapeDtypeStruct(shape, F32), jax.S...  83.8 us
    unnamed x4, local copies, waits for them, and re-layouts  2.34 us

profile of v3, /device:TPU:1, one launch (start us, length us, event | category | flops | bytes accessed | tf_op | source)
XLA Modules:
  0.0 86.8 jit_solution(4716905216294832661)
XLA Ops:
  0.6 83.8 %shard_map.122 = (f32[8,3,16,128]{3,2,1,0:T(8,128)}, f32[8,3,16,128]{3,2,1,0:T(8,128)}) custom-call(f32[8,3,16,128]{3,2,1,0:T(8,128)} %right_in.1, f32[8,3,16,128]{3,2,1,0:T(8,128)} %guess_in.1, bf16[8,3,3,16,128]{4,3,2,1,0:T(8,128)(2,1)} %diag_in.1, bf16[8,3,3,16,128]{4,3,2,1,0:T(8,128)(2,1)} %mob_in.1, bf16[6,8,16,128]{3,2,1,0:T(8,128)(2,1)} %face_in.1, ...), custom_call_target="tpu_custom_call" | custom-call | tf_op jit(solution)/shard_map/pallas_call | solution.py:506
  84.5 0.0 copy-start
  84.5 1.7 %copy.15 = f32[8,3,16,128]{3,2,1,0:T(8,128)} copy(f32[8,3,16,128]{3,2,1,0:T(8,128)} %get-tuple-element.4) | data formatting | bytes 393216
  86.1 0.0 copy-done
  86.1 0.7 copy.16
Async XLA Ops:
  84.5 1.7 %copy-start = (f32[8,3,16,128]{3,2,1,0:T(8,128)S(1)}, f32[8,3,16,128]{3,2,1,0:T(8,128)}, u32[]{:S(2)}) copy-start(f32[8,3,16,128]{3,2,1,0:T(8,128)} %get-tuple-element.5) | copy-start | bytes 589828

commit v4 on v3

--- a/solution.py
+++ b/solution.py
@@ -44,7 +44,7 @@
     right_ref, guess_ref, diag_ref, mob_ref, face_ref, colinv_ref, cell_ref, slot_ref, win_ref,
     wout_ref, winv_ref, load_sem,
     snd, rcv, flux_pad, col_snd, col_rcv, mt, faces, oht, cmt, cmb, terms, gts, gt, wmask, solver, vals, coef, link,
-    link_w, link_a, link_out,
+    link_w, link_a, link_out, own_in,
     snd_sem, rcv_sem, hs_sem, hr_sem,
 ):
     gx = lax.axis_index("gx")
@@ -96,12 +96,15 @@
         every_peer(one)
         rcv[index, pl.ds(me, 1), :] = snd[index, pl.ds(me, 1), :]
 
-    def receive(index):
+    def receive_wide(index):
         rows = pl.ds(0, DEV - 1)
         pltpu.make_async_copy(
             snd.at[index, rows], rcv.at[index, rows], rcv_sem.at[index]
         ).wait()
         return rcv[index].T
+
+    def receive(index):
+        return receive_wide(index)
 
     def sent(index):
         rows = pl.ds(0, DEV - 1)
@@ -276,68 +279,6 @@
 
     def combine(scale, xs, ys):
         return [x + scale * y for x, y in zip(xs, ys)]
-
-    loads["guess"].wait()
-    guess = [flat(guess_ref[:, c]) for c in range(3)]
-    gather(guess)
-    mt[0:48, :] = vals[...]
-    snd[0] = mt[...].T
-    pl.semaphore_wait(barrier, DEV - 1)
-    send(0)
-    for name in ("win", "wout", "mob", "diag", "right", "colinv"):
-        loads[name].wait()
-    inner = lax.bitwise_and(sub, 15)
-    layer = lax.shift_right_logical(sub, 4)
-    outside = (
-        (inner == 0) & (gx == 0),
-        (inner == 15) & (gx == 3),
-        (lane == 0) & (gy == 0),
-        (lane == 127) & (gy == 31),
-        layer == 0,
-        layer == 7,
-    )
-    loads["face"].wait()
-    for n in range(6):
-        faces[n] = jnp.where(outside[n], 0.0, flat(face_ref[n].astype(F32)))
-
-    started = stencil_start(0, guess)
-    loads["slot"].wait()
-    slots = slot_ref[:, 0, :]
-    well_of = lax.shift_right_logical(slots, 7)
-    seg_of = lax.bitwise_and(slots, 127)
-    for q in range(CAP):
-        part = slice(q * 128, (q + 1) * 128)
-        seg_hot = jnp.where(sub == seg_of[q : q + 1], 1.0, 0.0)
-        gt[:, part] = seg_hot.astype(BF16)
-        gts[part, :] = seg_hot.T.astype(BF16)
-        wmask[:, part] = jnp.where(sub8 == well_of[q : q + 1], 1.0, 0.0)
-    loads["winv"].wait()
-    fused = None
-    for w in range(8):
-        high, low = split(winv_ref[w].T)
-        rows = dot(high.astype(BF16), gt[...]) + dot(low.astype(BF16), gt[...])
-        rows = rows * wmask[w : w + 1, :]
-        fused = rows if fused is None else fused + rows
-    high, low = split(fused)
-    solver[0:128, :] = high.astype(BF16)
-    solver[128:256, :] = low.astype(BF16)
-
-    rows = [win_ref[c : c + 1, w * 128 : (w + 1) * 128] for c in range(3) for w in range(8)]
-    rows += [wout_ref[c : c + 1, w * 128 : (w + 1) * 128] for c in range(3) for w in range(8)]
-    own = by_slot(jnp.concatenate(rows, axis=0))
-    mt[...] = jnp.zeros((128, 128), F32)
-    for n in range(6):
-        put_rows(mt, 16 + n * 16, own[n])
-    got = receive(0)
-    rate = sum(mt[16 + 16 * c : 32 + 16 * c, :] * got[16 * c : 16 * c + 16] for c in range(3))
-    solve_wells(rate)
-    post(1)
-    applied = stencil_end(0, *started)
-    got = receive(1)
-    for n in range(6):
-        coef[n] = got[16 + 16 * n : 32 + 16 * n]
-    term = scatter(got[0:16])
-    r0 = [flat(right_ref[:, c]) - (applied[c] - term[c]) for c in range(3)]
 
     def rates_of(fields):
         gather(fields)
@@ -407,12 +348,80 @@
         term = scatter(back)
         return [applied[c] - term[c] for c in range(3)]
 
+    loads["guess"].wait()
+    guess = [flat(guess_ref[:, c]) for c in range(3)]
+    gather(guess)
+    for c in range(3):
+        mt[CAP * c : CAP * (c + 1), :] = vals[16 * c : 16 * c + CAP]
+    loads["slot"].wait()
+    slots = slot_ref[:, 0, :]
+    well_of = lax.shift_right_logical(slots, 7)
+    seg_of = lax.bitwise_and(slots, 127)
+    for q in range(CAP):
+        part = slice(q * 128, (q + 1) * 128)
+        seg_hot = jnp.where(sub == seg_of[q : q + 1], 1.0, 0.0)
+        gt[:, part] = seg_hot.astype(BF16)
+        gts[part, :] = seg_hot.T.astype(BF16)
+        wmask[:, part] = jnp.where(sub8 == well_of[q : q + 1], 1.0, 0.0)
+    for name in ("win", "wout"):
+        loads[name].wait()
+    rows = [ref[c : c + 1, w * 128 : (w + 1) * 128] for ref in (win_ref, wout_ref) for c in range(3) for w in range(8)]
+    own = by_slot(jnp.concatenate(rows, axis=0))
+    for n in range(6):
+        put_rows(mt, (3 + n) * CAP, own[n])
+    for c in range(3):
+        put_rows(own_in, c * 16, own[c])
+    snd[0] = mt[...].T
+    pl.semaphore_wait(barrier, DEV - 1)
+    send(0)
+    for name in ("mob", "diag", "right", "colinv"):
+        loads[name].wait()
+    inner = lax.bitwise_and(sub, 15)
+    layer = lax.shift_right_logical(sub, 4)
+    outside = (
+        (inner == 0) & (gx == 0),
+        (inner == 15) & (gx == 3),
+        (lane == 0) & (gy == 0),
+        (lane == 127) & (gy == 31),
+        layer == 0,
+        layer == 7,
+    )
+    loads["face"].wait()
+    for n in range(6):
+        faces[n] = jnp.where(outside[n], 0.0, flat(face_ref[n].astype(F32)))
+
+    started = stencil_start(0, guess)
+    loads["winv"].wait()
+    fused = None
+    for w in range(8):
+        high, low = split(winv_ref[w].T)
+        rows = dot(high.astype(BF16), gt[...]) + dot(low.astype(BF16), gt[...])
+        rows = rows * wmask[w : w + 1, :]
+        fused = rows if fused is None else fused + rows
+    high, low = split(fused)
+    solver[0:128, :] = high.astype(BF16)
+    solver[128:256, :] = low.astype(BF16)
+
+    coef[...] = jnp.zeros((6, 16, 128), F32)
     link_out[...] = jnp.zeros((16, 128), F32)
+    got = receive_wide(0)
+    mt[...] = jnp.zeros((128, 128), F32)
+    solve_wells(sum(own_in[16 * c : 16 * c + CAP, :] * got[CAP * c : CAP * (c + 1)] for c in range(3)))
+    post(1)
+    for n in range(6):
+        coef[n, 0:CAP, :] = got[(3 + n) * CAP : (4 + n) * CAP]
+
+    applied = stencil_end(0, *started)
+    part0 = [flat(right_ref[:, c]) - applied[c] for c in range(3)]
+    rates_d = rates_of(precondition(part0))
+    build_link()
+    got = receive(1)
+    mt[0:16, :] = rates_d + linked(1)
+    post(2)
+    term = scatter(got[0:16])
+    r0 = [part0[c] + term[c] for c in range(3)]
     u1 = precondition(r0)
-    mt[0:16, :] = rates_of(u1)
-    post(2)
     started = stencil_start(1, u1)
-    build_link()
     gather(r0)
     r0_out = coef[3] * vals[0:16] + coef[4] * vals[16:32] + coef[5] * vals[32:48]
     own_rho = local_sum(r0, r0)
@@ -532,6 +541,7 @@
             pltpu.VMEM((32, SLOTS), F32),
             pltpu.VMEM((128, 128), F32),
             pltpu.VMEM((16, 128), F32),
+            pltpu.VMEM((48, 128), F32),
             pltpu.SemaphoreType.DMA((EXCHANGES,)),
             pltpu.SemaphoreType.DMA((EXCHANGES,)),
             pltpu.SemaphoreType.DMA((OPS, 4)),

time: 87 us -> 85.8 us (0.986)
  Pallas kernels: 83.8 us -> 82.7 us
    pallas_call x1, Pallas kernels: 83.8 us -> 82.7 us  [per_device(): pl.pallas_call(kernel, out_shape=(jax.ShapeDtypeStruct(shape, F32), jax.S...]
where the time goes in v4:
time: 85.8 us; the launch traced here: 85.7 us
  Pallas kernels  82.7 us (96%)
  local copies, waits for them, and re-layouts  2.34 us (3%)
    pallas_call x1, Pallas kernels, per_device(): pl.pallas_call(kernel, out_shape=(jax.ShapeDtypeStruct(shape, F32), jax.S...  82.7 us
    unnamed x4, local copies, waits for them, and re-layouts  2.34 us

profile of v4, /device:TPU:1, one launch (start us, length us, event | category | flops | bytes accessed | tf_op | source)
XLA Modules:
  0.0 85.7 jit_solution(13473251860785532033)
XLA Ops:
  0.6 82.7 %shard_map.122 = (f32[8,3,16,128]{3,2,1,0:T(8,128)}, f32[8,3,16,128]{3,2,1,0:T(8,128)}) custom-call(f32[8,3,16,128]{3,2,1,0:T(8,128)} %right_in.1, f32[8,3,16,128]{3,2,1,0:T(8,128)} %guess_in.1, bf16[8,3,3,16,128]{4,3,2,1,0:T(8,128)(2,1)} %diag_in.1, bf16[8,3,3,16,128]{4,3,2,1,0:T(8,128)(2,1)} %mob_in.1, bf16[6,8,16,128]{3,2,1,0:T(8,128)(2,1)} %face_in.1, ...), custom_call_target="tpu_custom_call" | custom-call | tf_op jit(solution)/shard_map/pallas_call | solution.py:515
  83.3 0.0 copy-start
  83.3 1.7 %copy.15 = f32[8,3,16,128]{3,2,1,0:T(8,128)} copy(f32[8,3,16,128]{3,2,1,0:T(8,128)} %get-tuple-element.4) | data formatting | bytes 393216
  85.0 0.0 copy-done
  85.0 0.7 copy.16
Async XLA Ops:
  83.3 1.7 %copy-start = (f32[8,3,16,128]{3,2,1,0:T(8,128)S(1)}, f32[8,3,16,128]{3,2,1,0:T(8,128)}, u32[]{:S(2)}) copy-start(f32[8,3,16,128]{3,2,1,0:T(8,128)} %get-tuple-element.5) | copy-start | bytes 589828

commit v5 on v4

--- a/solution.py
+++ b/solution.py
@@ -96,15 +96,15 @@
         every_peer(one)
         rcv[index, pl.ds(me, 1), :] = snd[index, pl.ds(me, 1), :]
 
-    def receive_wide(index):
+    def arrive(index):
         rows = pl.ds(0, DEV - 1)
         pltpu.make_async_copy(
             snd.at[index, rows], rcv.at[index, rows], rcv_sem.at[index]
         ).wait()
+
+    def receive(index):
+        arrive(index)
         return rcv[index].T
-
-    def receive(index):
-        return receive_wide(index)
 
     def sent(index):
         rows = pl.ds(0, DEV - 1)
@@ -404,7 +404,7 @@
 
     coef[...] = jnp.zeros((6, 16, 128), F32)
     link_out[...] = jnp.zeros((16, 128), F32)
-    got = receive_wide(0)
+    got = receive(0)
     mt[...] = jnp.zeros((128, 128), F32)
     solve_wells(sum(own_in[16 * c : 16 * c + CAP, :] * got[CAP * c : CAP * (c + 1)] for c in range(3)))
     post(1)
@@ -487,22 +487,25 @@
     s1 = combine(-alpha1, r1, v1)
     got = receive(9)
     t1 = combine(-alpha1, a_r1, minus_wells(d4, got[0:16]))
-    post(10, [local_sum(t1, s1), local_sum(t1, t1)])
+    snd[10] = jnp.where(lane == 16, local_sum(t1, s1), jnp.where(lane == 17, local_sum(t1, t1), 0.0))
+    send(10)
     ms0 = combine(-alpha0, u1, u2)
     mr1 = combine(-omega0, ms0, u3)
     mp1 = combine(beta, mr1, combine(-omega0, u1, u2))
     ms1 = combine(-alpha1, mr1, u4)
     guess = [flat(guess_ref[:, c]) for c in range(3)]
     partial = combine(alpha1, combine(omega0, combine(alpha0, guess, u1), ms0), mp1)
-    got = receive(10)
-    omega1 = lane_sum(got, 0) / lane_sum(got, 1)
+    for index in range(EXCHANGES - 1):
+        sent(index)
+    arrive(10)
+    sums = jnp.sum(rcv[10], axis=0, keepdims=True)
+    omega1 = sums[:, 16:17] / sums[:, 17:18]
     final = combine(omega1, partial, ms1)
     left = combine(-omega1, s1, t1)
     for c in range(3):
         sol_ref[:, c] = final[c].reshape(8, 16, 128)
         res_ref[:, c] = left[c].reshape(8, 16, 128)
-    for index in range(EXCHANGES):
-        sent(index)
+    sent(10)
 
 
 def per_device(*args):

time: 85.8 us -> 85.7 us (level)
  no operation moved by 1% of the time
where the time goes in v5:
time: 85.7 us; the launch traced here: 85.5 us
  Pallas kernels  82.5 us (96%)
  local copies, waits for them, and re-layouts  2.34 us (3%)
    pallas_call x1, Pallas kernels, per_device(): pl.pallas_call(kernel, out_shape=(jax.ShapeDtypeStruct(shape, F32), jax.S...  82.5 us
    unnamed x4, local copies, waits for them, and re-layouts  2.34 us

profile of v5, /device:TPU:1, one launch (start us, length us, event | category | flops | bytes accessed | tf_op | source)
XLA Modules:
  0.0 85.5 jit_solution(4614159261364793314)
XLA Ops:
  0.6 82.5 %shard_map.122 = (f32[8,3,16,128]{3,2,1,0:T(8,128)}, f32[8,3,16,128]{3,2,1,0:T(8,128)}) custom-call(f32[8,3,16,128]{3,2,1,0:T(8,128)} %right_in.1, f32[8,3,16,128]{3,2,1,0:T(8,128)} %guess_in.1, bf16[8,3,3,16,128]{4,3,2,1,0:T(8,128)(2,1)} %diag_in.1, bf16[8,3,3,16,128]{4,3,2,1,0:T(8,128)(2,1)} %mob_in.1, bf16[6,8,16,128]{3,2,1,0:T(8,128)(2,1)} %face_in.1, ...), custom_call_target="tpu_custom_call" | custom-call | tf_op jit(solution)/shard_map/pallas_call | solution.py:518
  83.2 0.0 copy-start
  83.2 1.7 %copy.15 = f32[8,3,16,128]{3,2,1,0:T(8,128)} copy(f32[8,3,16,128]{3,2,1,0:T(8,128)} %get-tuple-element.4) | data formatting | bytes 393216
  84.9 0.0 copy-done
  84.9 0.7 copy.16
Async XLA Ops:
  83.2 1.7 %copy-start = (f32[8,3,16,128]{3,2,1,0:T(8,128)S(1)}, f32[8,3,16,128]{3,2,1,0:T(8,128)}, u32[]{:S(2)}) copy-start(f32[8,3,16,128]{3,2,1,0:T(8,128)} %get-tuple-element.5) | copy-start | bytes 589828
